TPU v7x, 512 devices: a whole 4x4x16 slice. The times are simulated.
512 devices in a mesh: band: 32 (over z, x_lo), member: 16 (over y, x_hi, core).
Axes of the slice: x: 4 (x_hi: 2, x_lo: 2; x = x_hi * 2 + x_lo), y: 4, z: 16, core: 2. Of those that a mesh axis runs over, the one named last changes fastest.
Arguments:
- tracer_mean: float32 [16, 4, 256, 768], P('member', None, 'band'), may hold values from -6 to 6
- slope_lon: float32 [16, 4, 256, 768], P('member', None, 'band'), may hold values from -3 to 3
- slope_lat: float32 [16, 4, 256, 768], P('member', None, 'band'), may hold values from -3 to 3
- zonal_courant: float32 [16, 4, 256, 768], P('member', None, 'band'), may hold values from -0.6 to 0.6
- merid_courant: float32 [16, 4, 256, 768], P('member', None, 'band'), may hold values from -0.6 to 0.6
- mixing: float32 [3, 256, 768], P(None, 'band'), may hold values from 0.1 to 3
- flux_map: float32 [256, 768], P('band'), may hold values from -6 to 6
- region: int32 [256, 768], P('band'), may hold values from 0 to 21
- scaling: float32 [16, 22], P('member'), may hold values from 0.5 to 2
- reader: int32 [32], P('band'), may hold values from 0 to 15
Outputs:
- new_mean: float32 [16, 4, 256, 768], P('member', None, 'band')
- new_slope_lon: float32 [16, 4, 256, 768], P('member', None, 'band')
- new_slope_lat: float32 [16, 4, 256, 768], P('member', None, 'band')
All inputs are finite; a program needn't handle non-finite values.
Results may differ from a plain program's by a relative error of at most 0.0003.
Values sent between devices are 32-bit elements; how exact they have to be, the bound alone decides.
A program may use at most 64 MiB of HBM per device.

v0:
```python
import jax
import jax.numpy as jnp
from jax import lax
from jax.sharding import PartitionSpec as P

SUB = 2


def spread(value, axis, source):
    kept = jnp.where(lax.axis_index(axis) == source, value, 0).astype(value.dtype)
    return lax.psum(kept, axis)


def window(field, start, size, axis):
    return lax.slice_in_dim(field, start, start + size, axis=axis)


def sweep(mean_ext, along_ext, cross_ext, faces, axis):
    count = mean_ext.shape[axis] - 2
    left_mean = window(mean_ext, 0, count + 1, axis)
    right_mean = window(mean_ext, 1, count + 1, axis)
    left_along = window(along_ext, 0, count + 1, axis)
    right_along = window(along_ext, 1, count + 1, axis)
    left_cross = window(cross_ext, 0, count + 1, axis)
    right_cross = window(cross_ext, 1, count + 1, axis)
    forward = faces > 0.0
    flux = jnp.where(
        forward,
        faces * (left_mean + 0.5 * (1.0 - faces) * left_along),
        faces * (right_mean - 0.5 * (1.0 + faces) * right_along),
    )
    along_flux = faces * jnp.where(forward, left_along, right_along)
    cross_flux = faces * jnp.where(forward, left_cross, right_cross)

    def divergence(values):
        return window(values, 0, count, axis) - window(values, 1, count, axis)

    new_mean = window(mean_ext, 1, count, axis) + divergence(flux)
    new_along = 0.5 * (window(along_ext, 1, count, axis) + divergence(along_flux)) + 0.25 * (
        window(mean_ext, 2, count, axis) - window(mean_ext, 0, count, axis)
    )
    new_cross = window(cross_ext, 1, count, axis) + divergence(cross_flux)
    return (new_mean, new_along, new_cross)


def extend_cycle(field):
    return jnp.concatenate([field[..., -1:], field, field[..., :1]], -1)


def extend_edge(field):
    return jnp.concatenate([field[..., :1, :], field, field[..., -1:, :]], -2)


def zonal_sweep(mean, along, cross, uwind):
    faces = jnp.concatenate([uwind, uwind[..., :1]], -1)
    return sweep(extend_cycle(mean), extend_cycle(along), extend_cycle(cross), faces, -1)


def vertical_mix(fields, mixing):
    levels = fields.shape[-3]
    zero = jnp.zeros_like(mixing[0])
    below = [zero] + [mixing[level - 1] for level in range(1, levels)]
    above = [mixing[level] for level in range(levels - 1)] + [zero]
    ratios = []
    values = []
    for level in range(levels):
        source = fields[..., level, :, :]
        denom = 1.0 + below[level] + above[level]
        if level > 0:
            denom = denom + below[level] * ratios[-1]
            source = source + below[level] * values[-1]
        ratios.append(-above[level] / denom)
        values.append(source / denom)
    result = [values[-1]]
    for level in range(levels - 2, -1, -1):
        result.append(values[level] - ratios[level] * result[-1])
    ordered = result[::-1]
    return jnp.stack(ordered, axis=-3)


def emission_of(flux_map, region, scaling):
    count = scaling.shape[-1]
    region_codes = jnp.arange(count, dtype=jnp.int32)
    onehot = (region[None] == region_codes[:, None, None]).astype(jnp.float32)
    weight = jnp.tensordot(scaling, onehot, axes=1, precision=lax.Precision.HIGHEST)
    land = jnp.where(region < count // 2, 1.0, 0.4)
    return 0.5 * flux_map * land * weight


def on_device(
    tracer_mean,
    slope_lon,
    slope_lat,
    zonal_courant,
    merid_courant,
    mixing,
    flux_map,
    region,
    scaling,
    reader,
):
    winds = spread(jnp.stack([zonal_courant[0], merid_courant[0]]), "member", reader[0])
    uwind = winds[0]
    lat_rows = winds.shape[2]
    band_index = lax.axis_index("band")
    global_rows = band_index * lat_rows + jnp.arange(lat_rows, dtype=jnp.int32)
    vwind = jnp.where(global_rows[None, :, None] > 0, winds[1], jnp.float32(0.0))
    mean = tracer_mean.at[:, 0].add(emission_of(flux_map, region, scaling))
    fields = vertical_mix(jnp.stack([mean, slope_lon, slope_lat]), mixing)
    mean, along_lon, along_lat = (fields[0], fields[1], fields[2])
    column_wind = lax.all_to_all(vwind, "band", split_axis=2, concat_axis=1, tiled=True)
    faces = jnp.concatenate([column_wind, jnp.zeros_like(column_wind[:, :1])], 1)
    for substep in range(SUB):
        mean, along_lon, along_lat = zonal_sweep(mean, along_lon, along_lat, uwind)
        mean, along_lon, along_lat = (
            lax.all_to_all(mean, "band", split_axis=3, concat_axis=2, tiled=True),
            lax.all_to_all(along_lon, "band", split_axis=3, concat_axis=2, tiled=True),
            lax.all_to_all(along_lat, "band", split_axis=3, concat_axis=2, tiled=True),
        )
        mean, along_lat, along_lon = sweep(
            extend_edge(mean), extend_edge(along_lat), extend_edge(along_lon), faces, -2
        )
        mean, along_lon, along_lat = (
            lax.all_to_all(mean, "band", split_axis=2, concat_axis=3, tiled=True),
            lax.all_to_all(along_lon, "band", split_axis=2, concat_axis=3, tiled=True),
            lax.all_to_all(along_lat, "band", split_axis=2, concat_axis=3, tiled=True),
        )
    return (mean, along_lon, along_lat)


def solution(mesh):
    return jax.shard_map(
        on_device,
        mesh=mesh,
        in_specs=(
            P("member", None, "band", None),
            P("member", None, "band", None),
            P("member", None, "band", None),
            P("member", None, "band", None),
            P("member", None, "band", None),
            P(None, "band", None),
            P("band", None),
            P("band", None),
            P("member", None),
            P("band"),
        ),
        out_specs=(
            P("member", None, "band", None),
            P("member", None, "band", None),
            P("member", None, "band", None),
        ),
        check_vma=False,
    )
```

profile of v0, /device:TPU:2, one launch (start us, length us, event | category | flops | bytes accessed | tf_op | source)
XLA Modules:
  0.0 451.0 jit_solution(14127448643584136338)
XLA Ops:
  14.3 149.1 %all-reduce.3.cloned.1.call-done = f32[2,4,8,768]{3,2,1,0:T(8,128)} async-done(((f32[2,4,8,768]{3,2,1,0:T(8,128)}), f32[2,4,8,768]{3,2,1,0:T(8,128)}) %all-reduce.3.cloned.1.call-update) | async-done | bytes 196624 | tf_op jit(solution)/shard_map/psum | solution.py:11
  165.5 2.4 reshape.1090
  167.9 13.8 %all-to-all-start.4 = ((f32[32,1,768]{2,1,0:T(1,128)}), f32[32,1,768]{2,1,0:T(1,128)S(1)}, u32[]{:S(2)}, u32[]{:S(2)}) async-start(f32[32,1,768]{2,1,0:T(1,128)} %reshape.1090), calls=%async_computation.4 | async-start | bytes 196608 | tf_op jit(solution)/shard_map/all_to_all | solution.py:117
  182.5 2.4 reshape.1086
  185.0 10.7 %all-to-all-done.4 = f32[32,1,768]{2,1,0:T(1,128)S(1)} async-done(((f32[32,1,768]{2,1,0:T(1,128)}), f32[32,1,768]{2,1,0:T(1,128)S(1)}, u32[]{:S(2)}, u32[]{:S(2)}) %all-to-all-start.4) | async-done | bytes 98336 | tf_op jit(solution)/shard_map/all_to_all | solution.py:117
  195.6 4.1 all-to-all-start.1
  200.4 2.4 reshape.1084
  202.9 10.9 %all-to-all-done.1 = f32[32,1,768]{2,1,0:T(1,128)S(1)} async-done(((f32[32,1,768]{2,1,0:T(1,128)}), f32[32,1,768]{2,1,0:T(1,128)S(1)}, u32[]{:S(2)}, u32[]{:S(2)}) %all-to-all-start.1) | async-done | bytes 98336 | tf_op jit(solution)/shard_map/all_to_all | solution.py:111
  213.7 4.4 all-to-all-start.2
  218.8 2.4 reshape.1082
  229.3 2.7 all-to-all-done.2
  232.0 10.5 %all-to-all-start = ((f32[32,1,768]{2,1,0:T(1,128)}), f32[32,1,768]{2,1,0:T(1,128)S(1)}, u32[]{:S(2)}, u32[]{:S(2)}) async-start(f32[32,1,768]{2,1,0:T(1,128)} %reshape.1082), calls=%async_computation | async-start | bytes 196608 | tf_op jit(solution)/shard_map/all_to_all | solution.py:116
  245.9 10.5 %all-to-all-done = f32[32,1,768]{2,1,0:T(1,128)S(1)} async-done(((f32[32,1,768]{2,1,0:T(1,128)}), f32[32,1,768]{2,1,0:T(1,128)S(1)}, u32[]{:S(2)}, u32[]{:S(2)}) %all-to-all-start) | async-done | bytes 98336 | tf_op jit(solution)/shard_map/all_to_all | solution.py:116
  263.2 4.1 all-to-all-start.7
  269.1 12.2 %all-to-all-done.7 = f32[32,1,768]{2,1,0:T(1,128)S(1)} async-done(((f32[32,1,768]{2,1,0:T(1,128)}), f32[32,1,768]{2,1,0:T(1,128)S(1)}, u32[]{:S(2)}, u32[]{:S(2)}) %all-to-all-start.7) | async-done | bytes 98336 | tf_op jit(solution)/shard_map/all_to_all | solution.py:126
  281.3 4.3 all-to-all-start.5
  287.4 12.3 %all-to-all-done.5 = f32[32,1,768]{2,1,0:T(1,128)S(1)} async-done(((f32[32,1,768]{2,1,0:T(1,128)}), f32[32,1,768]{2,1,0:T(1,128)S(1)}, u32[]{:S(2)}, u32[]{:S(2)}) %all-to-all-start.5) | async-done | bytes 98336 | tf_op jit(solution)/shard_map/all_to_all | solution.py:125
  299.7 4.2 all-to-all-start.3
  308.3 9.5 %all-to-all-done.3 = f32[32,1,768]{2,1,0:T(1,128)S(1)} async-done(((f32[32,1,768]{2,1,0:T(1,128)}), f32[32,1,768]{2,1,0:T(1,128)S(1)}, u32[]{:S(2)}, u32[]{:S(2)}) %all-to-all-start.3) | async-done | bytes 98336 | tf_op jit(solution)/shard_map/all_to_all | solution.py:124
  321.0 2.4 reshape.1102
  323.5 4.1 all-to-all-start.10
  331.0 10.5 %all-to-all-done.10 = f32[32,1,768]{2,1,0:T(1,128)S(1)} async-done(((f32[32,1,768]{2,1,0:T(1,128)}), f32[32,1,768]{2,1,0:T(1,128)S(1)}, u32[]{:S(2)}, u32[]{:S(2)}) %all-to-all-start.10) | async-done | bytes 98336 | tf_op jit(solution)/shard_map/all_to_all | solution.py:117
  341.5 4.7 %all-to-all-start.8 = ((f32[32,1,768]{2,1,0:T(1,128)}), f32[32,1,768]{2,1,0:T(1,128)S(1)}, u32[]{:S(2)}, u32[]{:S(2)}) async-start(f32[32,1,768]{2,1,0:T(1,128)} %reshape.1098), calls=%async_computation.8 | async-start | bytes 196608 | tf_op jit(solution)/shard_map/all_to_all | solution.py:118
  352.7 7.3 %all-to-all-done.8 = f32[32,1,768]{2,1,0:T(1,128)S(1)} async-done(((f32[32,1,768]{2,1,0:T(1,128)}), f32[32,1,768]{2,1,0:T(1,128)S(1)}, u32[]{:S(2)}, u32[]{:S(2)}) %all-to-all-start.8) | async-done | bytes 98336 | tf_op jit(solution)/shard_map/all_to_all | solution.py:118
  360.0 5.9 %all-to-all-start.6 = ((f32[32,1,768]{2,1,0:T(1,128)}), f32[32,1,768]{2,1,0:T(1,128)S(1)}, u32[]{:S(2)}, u32[]{:S(2)}) async-start(f32[32,1,768]{2,1,0:T(1,128)} %reshape.1094), calls=%async_computation.6 | async-start | bytes 196608 | tf_op jit(solution)/shard_map/all_to_all | solution.py:116
  369.4 10.5 %all-to-all-done.6 = f32[32,1,768]{2,1,0:T(1,128)S(1)} async-done(((f32[32,1,768]{2,1,0:T(1,128)}), f32[32,1,768]{2,1,0:T(1,128)S(1)}, u32[]{:S(2)}, u32[]{:S(2)}) %all-to-all-start.6) | async-done | bytes 98336 | tf_op jit(solution)/shard_map/all_to_all | solution.py:116
  386.7 4.1 all-to-all-start.12
  392.5 12.2 %all-to-all-done.12 = f32[32,1,768]{2,1,0:T(1,128)S(1)} async-done(((f32[32,1,768]{2,1,0:T(1,128)}), f32[32,1,768]{2,1,0:T(1,128)S(1)}, u32[]{:S(2)}, u32[]{:S(2)}) %all-to-all-start.12) | async-done | bytes 98336 | tf_op jit(solution)/shard_map/all_to_all | solution.py:126
  404.7 4.1 all-to-all-start.11
  410.6 12.3 %all-to-all-done.11 = f32[32,1,768]{2,1,0:T(1,128)S(1)} async-done(((f32[32,1,768]{2,1,0:T(1,128)}), f32[32,1,768]{2,1,0:T(1,128)S(1)}, u32[]{:S(2)}, u32[]{:S(2)}) %all-to-all-start.11) | async-done | bytes 98336 | tf_op jit(solution)/shard_map/all_to_all | solution.py:125
  422.9 4.3 all-to-all-start.9
  432.5 8.6 %all-to-all-done.9 = f32[32,1,768]{2,1,0:T(1,128)S(1)} async-done(((f32[32,1,768]{2,1,0:T(1,128)}), f32[32,1,768]{2,1,0:T(1,128)S(1)}, u32[]{:S(2)}, u32[]{:S(2)}) %all-to-all-start.9) | async-done | bytes 98336 | tf_op jit(solution)/shard_map/all_to_all | solution.py:124
  (124 shorter events, 71.3 us)
Async XLA Ops:
  7.2 5.8 %copy-start = (f32[1,22]{1,0:T(1,128)S(1)}, f32[1,22]{1,0:T(1,128)}, u32[]{:S(2)}) copy-start(f32[1,22]{1,0:T(1,128)} %param.20) | copy-start | bytes 268
  7.2 6.0 %copy-start.4 = (s32[8,768]{1,0:T(8,128)S(1)}, s32[8,768]{1,0:T(8,128)}, u32[]{:S(2)}) copy-start(s32[8,768]{1,0:T(8,128)} %param.19) | copy-start | bytes 73732
  7.2 6.0 %copy-start.5 = (f32[8,768]{1,0:T(8,128)S(1)}, f32[8,768]{1,0:T(8,128)}, u32[]{:S(2)}) copy-start(f32[8,768]{1,0:T(8,128)} %param.18) | copy-start | bytes 73732
  7.2 6.8 %copy-start.2 = (f32[1,4,8,768]{3,2,1,0:T(8,128)S(1)}, f32[1,4,8,768]{3,2,1,0:T(8,128)}, u32[]{:S(2)}) copy-start(f32[1,4,8,768]{3,2,1,0:T(8,128)} %param.14) | copy-start | bytes 294916
  7.2 6.8 %copy-start.3 = (f32[1,4,8,768]{3,2,1,0:T(8,128)S(1)}, f32[1,4,8,768]{3,2,1,0:T(8,128)}, u32[]{:S(2)}) copy-start(f32[1,4,8,768]{3,2,1,0:T(8,128)} %param.13) | copy-start | bytes 294916
  7.2 156.2 %all-reduce.3.cloned.1.call-start = ((), (), s32[]{:S(2)}) async-start(), calls=%async_computation.13 | async-start | bytes 393216 | tf_op jit(solution)/shard_map/psum | solution.py:11
  164.8 17.0 %copy-start.1 = (f32[2,4,8,768]{3,2,1,0:T(8,128)S(1)}, f32[2,4,8,768]{3,2,1,0:T(8,128)}, u32[]{:S(2)}) copy-start(f32[2,4,8,768]{3,2,1,0:T(8,128)} %all-reduce.3.cloned.1.call-done) | copy-start | bytes 589828
  167.9 27.7 %all-to-all-start.4 = ((f32[32,1,768]{2,1,0:T(1,128)}), f32[32,1,768]{2,1,0:T(1,128)S(1)}, u32[]{:S(2)}, u32[]{:S(2)}) async-start(f32[32,1,768]{2,1,0:T(1,128)} %reshape.1090), calls=%async_computation.4 | async-start | bytes 196608 | tf_op jit(solution)/shard_map/all_to_all | solution.py:117
  195.6 18.1 %all-to-all-start.1 = ((f32[32,1,768]{2,1,0:T(1,128)}), f32[32,1,768]{2,1,0:T(1,128)S(1)}, u32[]{:S(2)}, u32[]{:S(2)}) async-start(f32[32,1,768]{2,1,0:T(1,128)} %reshape.1086), calls=%async_computation.1 | async-start | bytes 196608 | tf_op jit(solution)/shard_map/all_to_all | solution.py:111
  213.7 18.2 %all-to-all-start.2 = ((f32[32,1,768]{2,1,0:T(1,128)}), f32[32,1,768]{2,1,0:T(1,128)S(1)}, u32[]{:S(2)}, u32[]{:S(2)}) async-start(f32[32,1,768]{2,1,0:T(1,128)} %reshape.1084), calls=%async_computation.2 | async-start | bytes 196608 | tf_op jit(solution)/shard_map/all_to_all | solution.py:118
  232.0 24.4 %all-to-all-start = ((f32[32,1,768]{2,1,0:T(1,128)}), f32[32,1,768]{2,1,0:T(1,128)S(1)}, u32[]{:S(2)}, u32[]{:S(2)}) async-start(f32[32,1,768]{2,1,0:T(1,128)} %reshape.1082), calls=%async_computation | async-start | bytes 196608 | tf_op jit(solution)/shard_map/all_to_all | solution.py:116
  263.2 18.0 %all-to-all-start.7 = ((f32[32,1,768]{2,1,0:T(1,128)}), f32[32,1,768]{2,1,0:T(1,128)S(1)}, u32[]{:S(2)}, u32[]{:S(2)}) async-start(f32[32,1,768]{2,1,0:T(1,128)} %reshape.1096), calls=%async_computation.7 | async-start | bytes 196608 | tf_op jit(solution)/shard_map/all_to_all | solution.py:126
  281.3 18.4 %all-to-all-start.5 = ((f32[32,1,768]{2,1,0:T(1,128)}), f32[32,1,768]{2,1,0:T(1,128)S(1)}, u32[]{:S(2)}, u32[]{:S(2)}) async-start(f32[32,1,768]{2,1,0:T(1,128)} %reshape.1092), calls=%async_computation.5 | async-start | bytes 196608 | tf_op jit(solution)/shard_map/all_to_all | solution.py:125
  299.7 18.1 %all-to-all-start.3 = ((f32[32,1,768]{2,1,0:T(1,128)}), f32[32,1,768]{2,1,0:T(1,128)S(1)}, u32[]{:S(2)}, u32[]{:S(2)}) async-start(f32[32,1,768]{2,1,0:T(1,128)} %reshape.1088), calls=%async_computation.3 | async-start | bytes 196608 | tf_op jit(solution)/shard_map/all_to_all | solution.py:124
  323.5 18.1 %all-to-all-start.10 = ((f32[32,1,768]{2,1,0:T(1,128)}), f32[32,1,768]{2,1,0:T(1,128)S(1)}, u32[]{:S(2)}, u32[]{:S(2)}) async-start(f32[32,1,768]{2,1,0:T(1,128)} %reshape.1102), calls=%async_computation.10 | async-start | bytes 196608 | tf_op jit(solution)/shard_map/all_to_all | solution.py:117
  341.5 18.5 %all-to-all-start.8 = ((f32[32,1,768]{2,1,0:T(1,128)}), f32[32,1,768]{2,1,0:T(1,128)S(1)}, u32[]{:S(2)}, u32[]{:S(2)}) async-start(f32[32,1,768]{2,1,0:T(1,128)} %reshape.1098), calls=%async_computation.8 | async-start | bytes 196608 | tf_op jit(solution)/shard_map/all_to_all | solution.py:118
  360.0 19.8 %all-to-all-start.6 = ((f32[32,1,768]{2,1,0:T(1,128)}), f32[32,1,768]{2,1,0:T(1,128)S(1)}, u32[]{:S(2)}, u32[]{:S(2)}) async-start(f32[32,1,768]{2,1,0:T(1,128)} %reshape.1094), calls=%async_computation.6 | async-start | bytes 196608 | tf_op jit(solution)/shard_map/all_to_all | solution.py:116
  386.7 18.0 %all-to-all-start.12 = ((f32[32,1,768]{2,1,0:T(1,128)}), f32[32,1,768]{2,1,0:T(1,128)S(1)}, u32[]{:S(2)}, u32[]{:S(2)}) async-start(f32[32,1,768]{2,1,0:T(1,128)} %reshape.1106), calls=%async_computation.12 | async-start | bytes 196608 | tf_op jit(solution)/shard_map/all_to_all | solution.py:126
  404.7 18.2 %all-to-all-start.11 = ((f32[32,1,768]{2,1,0:T(1,128)}), f32[32,1,768]{2,1,0:T(1,128)S(1)}, u32[]{:S(2)}, u32[]{:S(2)}) async-start(f32[32,1,768]{2,1,0:T(1,128)} %reshape.1104), calls=%async_computation.11 | async-start | bytes 196608 | tf_op jit(solution)/shard_map/all_to_all | solution.py:125
  422.9 18.3 %all-to-all-start.9 = ((f32[32,1,768]{2,1,0:T(1,128)}), f32[32,1,768]{2,1,0:T(1,128)S(1)}, u32[]{:S(2)}, u32[]{:S(2)}) async-start(f32[32,1,768]{2,1,0:T(1,128)} %reshape.1100), calls=%async_computation.9 | async-start | bytes 196608 | tf_op jit(solution)/shard_map/all_to_all | solution.py:124
Sparse Core Ops, SparseCore 0:
  11.0 152.3 all-reduce.2
where the time goes:
time: 459 us; the launch traced here: 451 us
  waiting for transfers between devices  279 us (61%)
  starting transfers between devices  72.7 us (16%)
  local copies, waits for them, and re-layouts  63 us (14%)
  other arithmetic  20.2 us (4%)
  between operations  15.7 us (3%)
    psum x1, waiting for transfers between devices, spread(): return lax.psum(kept, axis)  149 us
    unnamed x39, local copies, waits for them, and re-layouts  43.1 us
    all_to_all x2, waiting for transfers between devices, on_device(): lax.all_to_all(along_lon, 'band', split_axis=2, concat_axis=3, tiled=True)  24.6 us
    all_to_all x2, waiting for transfers between devices, on_device(): lax.all_to_all(along_lat, 'band', split_axis=2, concat_axis=3, tiled=True)  24.4 us
    all_to_all x2, waiting for transfers between devices, on_device(): lax.all_to_all(along_lon, 'band', split_axis=3, concat_axis=2, tiled=True)  21.2 us
    all_to_all x2, waiting for transfers between devices, on_device(): lax.all_to_all(mean, 'band', split_axis=3, concat_axis=2, tiled=True)  20.9 us
    all_to_all x2, waiting for transfers between devices, on_device(): lax.all_to_all(mean, 'band', split_axis=2, concat_axis=3, tiled=True)  18.1 us
    all_to_all x2, starting transfers between devices, on_device(): lax.all_to_all(along_lon, 'band', split_axis=3, concat_axis=2, tiled=True)  17.9 us
  transfers between devices with their start and end apart: 14, of which 14 were waited for; matrix products, arithmetic and copies ran while one was open for 12% of the time, Pallas kernels for 0%

commit v1 on v0

v1 whole, which is shorter than its diff:
```python
import jax
import jax.numpy as jnp
from jax import lax
from jax.experimental import pallas as pl
from jax.experimental.pallas import tpu as pltpu
from jax.sharding import PartitionSpec as P

SUB = 2
MESH = pl.DeviceIdType.MESH
LEVELS, ROWS, LONS = 4, 8, 768
MEMBERS, CHIPS, HALF = 16, 8, 384


def upwind(faces, left, right):
    forward = faces > 0.0
    mean, along, cross = (jnp.where(forward, l, r) for l, r in zip(left, right))
    weight = 0.5 * (jnp.where(forward, 1.0, -1.0) - faces)
    return faces * (mean + weight * along), faces * along, faces * cross


def advance(cells, flux, flux_next, mean_prev, mean_next):
    mean, along, cross = cells
    return (
        mean + (flux[0] - flux_next[0]),
        0.5 * (along + (flux[1] - flux_next[1])) + 0.25 * (mean_next - mean_prev),
        cross + (flux[2] - flux_next[2]),
    )


def zonal(cells, faces):
    count = faces.shape[-1]
    left = tuple(pltpu.roll(x, 1, 1) for x in cells)
    flux = upwind(faces, left, cells)
    flux_next = tuple(pltpu.roll(x, count - 1, 1) for x in flux)
    return advance(cells, flux, flux_next, left[0], pltpu.roll(cells[0], count - 1, 1))


def kernel(
    mean_h, lon_h, lat_h, zon_h, mer_h, mix_h, flux_h, region_h, scaling_s, reader_s,
    out_mean, out_lon, out_lat,
    cells, mix_v, flux_v, region_v, got, winds, pack, halo, edge,
    in_sem, own_sem, scatter_send, scatter_recv, gather_send, gather_recv,
    halo_send, halo_recv, out_sem,
):
    band, me = lax.axis_index("band"), lax.axis_index("member")
    bands = lax.axis_size("band")
    chip, core = me // 2, me % 2
    has_south, has_north = band > 0, band < bands - 1

    loads = [
        pltpu.make_async_copy(mix_h, mix_v, in_sem.at[3]),
        pltpu.make_async_copy(flux_h, flux_v, in_sem.at[4]),
        pltpu.make_async_copy(region_h, region_v, in_sem.at[5]),
        pltpu.make_async_copy(mean_h.at[0], cells.at[0], in_sem.at[0]),
        pltpu.make_async_copy(lon_h.at[0], cells.at[1], in_sem.at[1]),
        pltpu.make_async_copy(lat_h.at[0], cells.at[2], in_sem.at[2]),
    ]
    for load in loads:
        load.start()

    barrier = pltpu.get_barrier_semaphore()
    for step in range(1, MEMBERS):
        pl.semaphore_signal(barrier, inc=1, device_id=(band, (me + step) % MEMBERS), device_id_type=MESH)

    @pl.when(has_south)
    def _():
        pl.semaphore_signal(barrier, inc=1, device_id=(band - 1, me), device_id_type=MESH)

    @pl.when(has_north)
    def _():
        pl.semaphore_signal(barrier, inc=1, device_id=(band + 1, me), device_id_type=MESH)

    pl.semaphore_wait(barrier, MEMBERS - 1 + has_south.astype(jnp.int32) + has_north.astype(jnp.int32))

    def piece(c, q):
        source = mer_h if c else zon_h
        return source.at[0, q // 2, :, pl.ds(pl.multiple_of((q % 2) * HALF, HALF), HALF)]

    for c in range(2):
        for d in range(CHIPS):
            q = (chip + d) % CHIPS
            slot = (2 * d + c - core + MEMBERS) % MEMBERS

            def send():
                pltpu.make_async_remote_copy(
                    src_ref=piece(c, q), dst_ref=got.at[slot], send_sem=scatter_send,
                    recv_sem=scatter_recv, device_id=(band, 2 * q + c), device_id_type=MESH,
                ).start()

            if d:
                send()
            else:
                pl.when(core != c)(send)

                @pl.when(core == c)
                def _():
                    pltpu.make_async_copy(piece(c, q), got.at[0], own_sem).start()

    for load in loads[:3]:
        load.wait()
    region = region_v[...]
    weight = jnp.zeros(region.shape, jnp.float32)
    for code in range(scaling_s.shape[1]):
        weight = jnp.where(region == code, scaling_s[0, code], weight)
    land = jnp.where(region < scaling_s.shape[1] // 2, 1.0, 0.4)
    emission = 0.5 * flux_v[...] * land * weight
    zero = jnp.zeros_like(emission)
    below = [zero] + [mix_v[level] for level in range(LEVELS - 1)]
    above = below[1:] + [zero]
    ratios, inverse = [], []
    for level in range(LEVELS):
        denom = 1.0 + below[level] + above[level]
        if level:
            denom = denom + below[level] * ratios[-1]
        inverse.append(1.0 / denom)
        ratios.append(-above[level] * inverse[-1])
    for load in loads[3:]:
        load.wait()
    for k in range(3):
        values = []
        for level in range(LEVELS):
            source = cells[k, level]
            if k == 0 and level == 0:
                source = source + emission
            if level:
                source = source + below[level] * values[-1]
            values.append(source * inverse[level])
        result = values[-1]
        cells[k, LEVELS - 1] = result
        for level in range(LEVELS - 2, -1, -1):
            result = values[level] - ratios[level] * result
            cells[k, level] = result

    pltpu.make_async_copy(piece(0, chip), got.at[0], own_sem).wait()
    rest = got.at[pl.ds(1, MEMBERS - 1)]
    pltpu.make_async_copy(rest, rest, scatter_recv).wait()
    winds[core, chip] = got[(me - reader_s[0] + MEMBERS) % MEMBERS]
    for step in range(1, MEMBERS):
        pltpu.make_async_remote_copy(
            src_ref=winds.at[core, chip], dst_ref=winds.at[core, chip], send_sem=gather_send,
            recv_sem=gather_recv.at[core], device_id=(band, (me + step) % MEMBERS), device_id_type=MESH,
        ).start()

    def await_winds(c):
        for count in (CHIPS - 1, CHIPS):
            @pl.when((core == c) == (count == CHIPS - 1))
            def _():
                part = winds.at[c, pl.ds(0, count)]
                pltpu.make_async_copy(part, part, gather_recv.at[c]).wait()

    def wind(c, level):
        return jnp.concatenate([winds[c, 2 * level], winds[c, 2 * level + 1]], -1)

    row = lax.broadcasted_iota(jnp.int32, (ROWS, LONS), 0)
    outs = (out_mean, out_lon, out_lat)

    for sub in range(SUB):
        if sub == 0:
            await_winds(0)
        for level in range(LEVELS):
            new = zonal((cells[0, level], cells[1, level], cells[2, level]), wind(0, level))
            for k in range(3):
                cells[k, level] = new[k]
                for side, r in ((0, 0), (1, ROWS - 1)):
                    pack[sub, side, pl.ds(k * LEVELS + level, 1), :] = new[k][r:r + 1]
        if sub == 0:
            await_winds(1)
        for level in range(LEVELS):
            v = wind(1, level)
            pack[sub, 0, pl.ds(3 * LEVELS + level, 1), :] = v[0:1]
            pack[sub, 1, pl.ds(3 * LEVELS + level, 1), :] = jnp.zeros((1, LONS), jnp.float32)

        def exchange(side):
            return pltpu.make_async_remote_copy(
                src_ref=pack.at[sub, side], dst_ref=halo.at[sub, 1 - side],
                send_sem=halo_send.at[sub, side], recv_sem=halo_recv.at[sub, 1 - side],
                device_id=(band + (1 if side else -1), me), device_id_type=MESH,
            )

        for side, there in ((0, has_south), (1, has_north)):
            pl.when(there)(exchange(side).start)

        for side, there in ((0, has_south), (1, has_north)):
            @pl.when(there)
            def _():
                exchange(1 - side).wait_recv()

            @pl.when(jnp.logical_not(there))
            def _():
                halo[sub, side] = pack[sub, side]
                halo[sub, side, pl.ds(3 * LEVELS, LEVELS), :] = jnp.zeros((LEVELS, LONS), jnp.float32)

        def packed(ref, side):
            return tuple(ref[sub, side, pl.ds(k * LEVELS, LEVELS), :] for k in (0, 2, 1))

        last = upwind(halo[sub, 1, pl.ds(3 * LEVELS, LEVELS), :], packed(pack, 1), packed(halo, 1))
        for k in range(3):
            edge[k] = last[k]

        for level in range(LEVELS):
            faces = wind(1, level)
            faces = jnp.where(jnp.logical_and(row == 0, band == 0), 0.0, faces)
            here = tuple(cells[k, level] for k in (0, 2, 1))
            south = [halo[sub, 0, pl.ds(k * LEVELS + level, 1), :] for k in (0, 2, 1)]
            left = tuple(
                jnp.where(row == 0, s, pltpu.roll(x, 1, 0)) for s, x in zip(south, here)
            )
            flux = upwind(faces, left, here)
            flux_next = tuple(
                jnp.where(row == ROWS - 1, edge[k, pl.ds(level, 1), :], pltpu.roll(flux[k], ROWS - 1, 0))
                for k in range(3)
            )
            mean_next = jnp.where(
                row == ROWS - 1, halo[sub, 1, pl.ds(level, 1), :], pltpu.roll(here[0], ROWS - 1, 0)
            )
            new = advance(here, flux, flux_next, left[0], mean_next)
            for k, value in zip((0, 2, 1), new):
                cells[k, level] = value

    stores = [pltpu.make_async_copy(cells.at[k], outs[k].at[0], out_sem.at[k]) for k in range(3)]
    for store in stores:
        store.start()
    pltpu.make_async_copy(rest, rest, scatter_send).wait()
    sent = got.at[pl.ds(1, MEMBERS - 1)]
    pltpu.make_async_copy(sent, sent, gather_send).wait()
    for sub in range(SUB):
        for side, there in ((0, has_south), (1, has_north)):
            @pl.when(there)
            def _():
                done = pack.at[sub, side]
                pltpu.make_async_copy(done, done, halo_send.at[sub, side]).wait()
    for store in stores:
        store.wait()


def on_device(*args):
    shape = jax.ShapeDtypeStruct(args[0].shape, jnp.float32)
    hbm = pl.BlockSpec(memory_space=pl.ANY)
    smem = pl.BlockSpec(memory_space=pltpu.SMEM)
    dma = pltpu.SemaphoreType.DMA
    vmem = lambda *dims: pltpu.VMEM(dims, jnp.float32)
    return pl.pallas_call(
        kernel,
        out_shape=(shape,) * 3,
        in_specs=[hbm] * 8 + [smem] * 2,
        out_specs=(hbm,) * 3,
        scratch_shapes=[
            vmem(3, LEVELS, ROWS, LONS),
            vmem(LEVELS - 1, ROWS, LONS),
            vmem(ROWS, LONS),
            pltpu.VMEM((ROWS, LONS), jnp.int32),
            vmem(MEMBERS, ROWS, HALF),
            vmem(2, CHIPS, ROWS, HALF),
            vmem(SUB, 2, 4 * LEVELS, LONS),
            vmem(SUB, 2, 4 * LEVELS, LONS),
            vmem(3, LEVELS, LONS),
            dma((6,)), dma, dma, dma, dma, dma((2,)), dma((SUB, 2)), dma((SUB, 2)), dma((3,)),
        ],
        compiler_params=pltpu.CompilerParams(collective_id=0, has_side_effects=True),
    )(*args)


def solution(mesh):
    moments = P("member", None, "band", None)
    return jax.shard_map(
        on_device,
        mesh=mesh,
        in_specs=(
            moments, moments, moments, moments, moments,
            P(None, "band", None),
            P("band", None),
            P("band", None),
            P("member", None),
            P("band"),
        ),
        out_specs=(moments,) * 3,
        check_vma=False,
    )
```

time: 459 us -> 33.2 us (0.07)
  the two profiles are of different devices: /device:TPU:2 before, /device:TPU:384 now
where the time goes in v1:
time: 33.2 us; the launch traced here: 32.9 us
  Pallas kernels  28.5 us (86%)
  local copies, waits for them, and re-layouts  3.15 us (9%)
  between operations  1.3 us (4%)
    pallas_call x1, Pallas kernels, on_device(): pl.pallas_call(kernel, out_shape=(shape,) * 3, in_specs=[hbm] * 8 + [smem...  28.5 us
    unnamed x7, local copies, waits for them, and re-layouts  3.15 us

profile of v1, /device:TPU:384, one launch (start us, length us, event | category | flops | bytes accessed | tf_op | source)
XLA Modules:
  0.0 32.9 jit_solution(8415031493789341708)
XLA Ops:
  1.3 28.5 %shard_map.121 = (f32[1,4,8,768]{3,2,1,0:T(8,128)}, f32[1,4,8,768]{3,2,1,0:T(8,128)}, f32[1,4,8,768]{3,2,1,0:T(8,128)}) custom-call(f32[1,4,8,768]{3,2,1,0:T(8,128)} %mean_h.1, f32[1,4,8,768]{3,2,1,0:T(8,128)} %lon_h.1, f32[1,4,8,768]{3,2,1,0:T(8,128)} %lat_h.1, f32[1,4,8,768]{3,2,1,0:T(8,128)} %zon_h.1, f32[1,4,8,768]{3,2,1,0:T(8,128)} %mer_h.1, ...), custom_call_target="tpu_custom_call" | custom-call | tf_op jit(solution)/shard_map/pallas_call | solution.py:242
  29.8 0.0 copy-start.1
  29.8 1.6 %copy.17 = f32[1,4,8,768]{3,2,1,0:T(8,128)} copy(f32[1,4,8,768]{3,2,1,0:T(8,128)} %get-tuple-element.6) | data formatting | bytes 196608
  31.3 0.0 copy-done.1
  31.4 0.0 copy-start
  31.4 0.6 %copy.18 = f32[1,4,8,768]{3,2,1,0:T(8,128)} copy(f32[1,4,8,768]{3,2,1,0:T(8,128)S(1)} %copy-done.1) | data formatting | bytes 196608
  32.0 0.3 copy-done
  32.3 0.6 %copy.19 = f32[1,4,8,768]{3,2,1,0:T(8,128)} copy(f32[1,4,8,768]{3,2,1,0:T(8,128)S(1)} %copy-done) | data formatting | bytes 196608
Async XLA Ops:
  29.8 1.6 %copy-start.1 = (f32[1,4,8,768]{3,2,1,0:T(8,128)S(1)}, f32[1,4,8,768]{3,2,1,0:T(8,128)}, u32[]{:S(2)}) copy-start(f32[1,4,8,768]{3,2,1,0:T(8,128)} %get-tuple-element.7) | copy-start | bytes 294916
  31.4 0.9 %copy-start = (f32[1,4,8,768]{3,2,1,0:T(8,128)S(1)}, f32[1,4,8,768]{3,2,1,0:T(8,128)}, u32[]{:S(2)}) copy-start(f32[1,4,8,768]{3,2,1,0:T(8,128)} %get-tuple-element.8) | copy-start | bytes 294916

commit v2 on v1

v2 whole, which is shorter than its diff:
```python
import jax
import jax.numpy as jnp
from jax import lax
from jax.experimental import pallas as pl
from jax.experimental.pallas import tpu as pltpu
from jax.sharding import PartitionSpec as P

SUB = 2
MESH = pl.DeviceIdType.MESH
LEVELS, ROWS, LONS, REGIONS = 4, 8, 768, 22
MEMBERS, CHIPS, HALF = 16, 8, 384
U, V = 3, 4
OFFSETS = ((2, 1), (1, 1), (3, 1), (2, 0), (0, 1), (1, 0), (3, 0), (0, 0))


def upwind(faces, left, right):
    forward = faces > 0.0
    mean, along, cross = (jnp.where(forward, l, r) for l, r in zip(left, right))
    weight = 0.5 * (jnp.where(forward, 1.0, -1.0) - faces)
    return faces * (mean + weight * along), faces * along, faces * cross


def advance(cells, flux, flux_next, mean_prev, mean_next):
    mean, along, cross = cells
    return (
        mean + (flux[0] - flux_next[0]),
        0.5 * (along + (flux[1] - flux_next[1])) + 0.25 * (mean_next - mean_prev),
        cross + (flux[2] - flux_next[2]),
    )


def zonal(cells, faces):
    count = faces.shape[-1]
    left = tuple(pltpu.roll(x, 1, 1) for x in cells)
    flux = upwind(faces, left, cells)
    flux_next = tuple(pltpu.roll(x, count - 1, 1) for x in flux)
    return advance(cells, flux, flux_next, left[0], pltpu.roll(cells[0], count - 1, 1))


def wind_of(winds, c, level):
    return jnp.concatenate([winds[c, 2 * level], winds[c, 2 * level + 1]], -1)


def exchange_kernel(
    mean_h, lon_h, lat_h, zon_h, mer_h, mix_h, flux_h, region_h, scaling_h, reader_h,
    cells, winds, halo,
    mix_v, flux_v, region_v, scaling_s, reader_s, got, pack,
    in_sem, own_sem, scatter_send, scatter_recv, gather_send, gather_recv,
    halo_send, halo_recv, late, beside,
):
    band, me = lax.axis_index("band"), lax.axis_index("member")
    bands = lax.axis_size("band")
    chip, core = me // 2, me % 2
    has_south, has_north = band > 0, band < bands - 1
    around = has_south.astype(jnp.int32) + has_north.astype(jnp.int32)
    tail_end = me == 0
    answers = jnp.logical_and(tail_end, band % 2 == 0)

    loads = [
        pltpu.make_async_copy(mix_h, mix_v, in_sem.at[3]),
        pltpu.make_async_copy(flux_h, flux_v, in_sem.at[4]),
        pltpu.make_async_copy(region_h, region_v, in_sem.at[5]),
        pltpu.make_async_copy(scaling_h, scaling_s, in_sem.at[6]),
        pltpu.make_async_copy(mean_h.at[0], cells.at[0], in_sem.at[0]),
        pltpu.make_async_copy(lon_h.at[0], cells.at[1], in_sem.at[1]),
        pltpu.make_async_copy(lat_h.at[0], cells.at[2], in_sem.at[2]),
    ]
    load_reader = pltpu.make_async_copy(reader_h, reader_s, in_sem.at[7])

    def signal_beside(semaphore):
        for there, step in ((has_south, -1), (has_north, 1)):
            @pl.when(there)
            def _():
                pl.semaphore_signal(semaphore, inc=1, device_id=(band + step, me), device_id_type=MESH)

    def signal_members(semaphore):
        for step in range(1, MEMBERS):
            pl.semaphore_signal(semaphore, inc=1, device_id=(band, (me + step) % MEMBERS), device_id_type=MESH)

    barrier = pltpu.get_barrier_semaphore()
    pl.when(jnp.logical_not(tail_end))(lambda: signal_members(barrier))
    pl.when(jnp.logical_not(answers))(lambda: signal_beside(barrier))
    pl.semaphore_wait(
        barrier,
        jnp.where(tail_end, jnp.where(answers, MEMBERS - 1 + around, MEMBERS - 1), MEMBERS - 2 + around),
    )

    def piece(c, q):
        source = mer_h if c else zon_h
        return source.at[0, q // 2, :, pl.ds(pl.multiple_of((q % 2) * HALF, HALF), HALF)]

    for dy, dx in OFFSETS:
        q = ((chip // 2 + dy) % 4) * 2 + (chip + dx) % 2
        for c in range(2):
            owner = jnp.maximum(2 * q + c, 1)
            spare = (owner != 2 * q + c).astype(jnp.int32)

            def send():
                pltpu.make_async_remote_copy(
                    src_ref=piece(c, q), dst_ref=got.at[spare, me], send_sem=scatter_send,
                    recv_sem=scatter_recv.at[spare], device_id=(band, owner), device_id_type=MESH,
                ).start()

            def keep():
                pltpu.make_async_copy(piece(c, q), got.at[spare, me], own_sem.at[spare]).start()

            if (dy, dx) == (0, 0):
                pl.when(owner != me)(send)
                pl.when(owner == me)(keep)
            else:
                send()

    load_reader.start()
    for load in loads:
        load.start()

    @pl.when(tail_end)
    def _():
        signal_members(late)

    pl.when(answers)(lambda: signal_beside(beside))

    for load in loads[:4]:
        load.wait()
    region = region_v[...]
    weight = jnp.zeros(region.shape, jnp.float32)
    for code in range(REGIONS):
        weight = jnp.where(region == code, scaling_s[0, code], weight)
    land = jnp.where(region < REGIONS // 2, 1.0, 0.4)
    emission = 0.5 * flux_v[...] * land * weight
    zero = jnp.zeros_like(emission)
    below = [zero] + [mix_v[level] for level in range(LEVELS - 1)]
    above = below[1:] + [zero]
    ratios, inverse = [], []
    for level in range(LEVELS):
        denom = 1.0 + below[level] + above[level]
        if level:
            denom = denom + below[level] * ratios[-1]
        inverse.append(1.0 / denom)
        ratios.append(-above[level] * inverse[-1])
    for load in loads[4:]:
        load.wait()
    for k in range(3):
        values = []
        for level in range(LEVELS):
            source = cells[k, level]
            if k == 0 and level == 0:
                source = source + emission
            if level:
                source = source + below[level] * values[-1]
            values.append(source * inverse[level])
        result = values[-1]
        for level in range(LEVELS - 1, -1, -1):
            if level < LEVELS - 1:
                result = values[level] - ratios[level] * result
            cells[k, level] = result
            pack[0, k, pl.ds(2 * level, 2), :] = result[:2]
            pack[1, k, pl.ds(2 * level, 2), :] = result[ROWS - 2:]

    def across(side, part, first, count):
        return pltpu.make_async_remote_copy(
            src_ref=pack.at[side, pl.ds(first, count)], dst_ref=halo.at[1 - side, pl.ds(first, count)],
            send_sem=halo_send.at[part, side], recv_sem=halo_recv.at[part, 1 - side],
            device_id=(band + (1 if side else -1), me), device_id_type=MESH,
        )

    parts = ((0, 3), (U, 1), (V, 1))
    sides = ((0, has_south), (1, has_north))

    def send_across(part):
        for side, there in sides:
            pl.when(there)(across(side, part, *parts[part]).start)

    load_reader.wait()

    @pl.when(jnp.logical_and(tail_end, jnp.logical_not(answers)))
    def _():
        pl.semaphore_wait(beside, around)

    send_across(0)

    most = got.at[0, pl.ds(0, MEMBERS - 1)]

    def arrive(spare):
        kept = got.at[spare, me]
        pltpu.make_async_copy(kept, kept, own_sem.at[spare]).wait()
        pltpu.make_async_copy(most, most, scatter_recv.at[spare]).wait()

    def pass_on(c, q, target):
        pltpu.make_async_remote_copy(
            src_ref=winds.at[c, q], dst_ref=winds.at[c, q], send_sem=gather_send,
            recv_sem=gather_recv.at[c], device_id=(band, target), device_id_type=MESH,
        ).start()

    @pl.when(jnp.logical_not(tail_end))
    def _():
        arrive(0)
        pl.when(me == 1)(lambda: arrive(1))
        winds[core, chip] = got[0, reader_s[0]]
        for dy, dx in OFFSETS:
            q = ((chip // 2 + dy) % 4) * 2 + (chip + dx) % 2
            for c in range(2):
                target = 2 * q + c

                @pl.when(jnp.logical_and(target != me, target != 0))
                def _():
                    pass_on(core, chip, target)

        pl.semaphore_wait(late, 1)
        pass_on(core, chip, 0)

    @pl.when(me == 1)
    def _():
        winds[0, 0] = got[1, reader_s[0]]
        for target in [*range(MEMBERS - 1, 1, -1), 0]:
            pass_on(0, 0, target)

    def await_winds(c):
        mine = jnp.logical_and(jnp.logical_not(tail_end), core == c)
        if c == 0:
            mine = jnp.logical_or(mine, me == 1)
        for count, case in ((CHIPS - 1, mine), (CHIPS, jnp.logical_not(mine))):
            @pl.when(case)
            def _():
                part = winds.at[c, pl.ds(0, count)]
                pltpu.make_async_copy(part, part, gather_recv.at[c]).wait()

    for c in range(2):
        await_winds(c)
        for level in range(LEVELS):
            rows = wind_of(winds, c, level)
            pack[0, U + c, pl.ds(2 * level, 2), :] = rows[:2]
            pack[1, U + c, pl.ds(2 * level, 2), :] = rows[ROWS - 2:]
        send_across(1 + c)

    for level in range(LEVELS):
        new = zonal((cells[0, level], cells[1, level], cells[2, level]), wind_of(winds, 0, level))
        for k in range(3):
            cells[k, level] = new[k]

    for side, there in sides:
        @pl.when(jnp.logical_not(there))
        def _():
            halo[side] = jnp.zeros((5, ROWS, LONS), jnp.float32)

    @pl.when(tail_end)
    def _():
        every = got.at[0]
        pltpu.make_async_copy(every, every, scatter_send).wait()

    @pl.when(jnp.logical_not(tail_end))
    def _():
        sent = got.at[0, pl.ds(0, MEMBERS - 1)]

        @pl.when(me == 1)
        def _():
            some = got.at[0, pl.ds(0, MEMBERS - 2)]
            pltpu.make_async_copy(some, some, scatter_send).wait()
            pltpu.make_async_copy(sent, sent, gather_send).wait()

        @pl.when(me != 1)
        def _():
            pltpu.make_async_copy(sent, sent, scatter_send).wait()

        pltpu.make_async_copy(sent, sent, gather_send).wait()

    for part in range(3):
        for side, there in sides:
            @pl.when(there)
            def _():
                across(side, part, *parts[part]).wait_send()
                across(1 - side, part, *parts[part]).wait_recv()


def finish_kernel(cells_in, winds, halo, out_mean, out_lon, out_lat, cells, edge, south, last, north, out_sem):
    band = lax.axis_index("band")
    bands = lax.axis_size("band")
    first_band, last_band = band == 0, band == bands - 1
    row = lax.broadcasted_iota(jnp.int32, (ROWS, LONS), 0)
    order = (0, 2, 1)
    outs = (out_mean, out_lon, out_lat)

    def up(x):
        return pltpu.roll(x, 1, 0)

    def down(x):
        return pltpu.roll(x, ROWS - 1, 0)

    def meridional(c):
        return (c[0], c[2], c[1])

    s_cells = tuple(halo[0, k] for k in range(3))
    n_cells = tuple(halo[1, k] for k in range(3))
    v_north = jnp.where(last_band, 0.0, halo[1, V])
    for level in range(LEVELS):
        edge[3, pl.ds(2 * level + 1, 1), :] = wind_of(winds, 1, level)[:1]
        edge[3, pl.ds(2 * level, 1), :] = jnp.zeros((1, LONS), jnp.float32)
    stores = []
    for sub in range(SUB):
        source = cells if sub else cells_in
        for level in range(LEVELS):
            here = tuple(source[k, level] for k in range(3))
            if sub:
                here = zonal(here, wind_of(winds, 0, level))
            for k in range(3):
                if sub:
                    cells[k, level] = here[k]
                edge[k, pl.ds(2 * level, 1), :] = here[k][ROWS - 1:]
                edge[k, pl.ds(2 * level + 1, 1), :] = here[k][:1]
        edges = tuple(edge[k] for k in range(3))
        s_cells = tuple(jnp.where(first_band, e, x) for e, x in zip(edges, zonal(s_cells, halo[0, U])))
        n_cells = tuple(jnp.where(last_band, e, x) for e, x in zip(edges, zonal(n_cells, halo[1, U])))
        s_mer, n_mer, e_mer = meridional(s_cells), meridional(n_cells), meridional(edges)
        flux_8 = upwind(v_north, e_mer, n_mer)
        for k in range(3):
            south[k] = s_mer[k]
            last[k] = flux_8[k]
        north[...] = n_cells[0]
        if sub < SUB - 1:
            flux_m1 = upwind(halo[0, V], tuple(up(x) for x in s_mer), s_mer)
            flux_0 = upwind(edge[3], s_mer, e_mer)
            s_cells = meridional(advance(s_mer, flux_m1, flux_0, up(s_mer[0]), e_mer[0]))
            flux_9 = upwind(down(v_north), n_mer, tuple(down(x) for x in n_mer))
            n_cells = meridional(advance(n_mer, flux_8, flux_9, e_mer[0], down(n_mer[0])))
        source = cells if sub else cells_in
        for level in range(LEVELS):
            faces = jnp.where(jnp.logical_and(row == 0, first_band), 0.0, wind_of(winds, 1, level))
            here = tuple(source[k, level] for k in order)
            left = tuple(
                jnp.where(row == 0, south[k, pl.ds(2 * level + 1, 1), :], up(x)) for k, x in enumerate(here)
            )
            flux = upwind(faces, left, here)
            flux_next = tuple(
                jnp.where(row == ROWS - 1, last[k, pl.ds(2 * level, 1), :], down(x)) for k, x in enumerate(flux)
            )
            mean_next = jnp.where(row == ROWS - 1, north[pl.ds(2 * level, 1), :], down(here[0]))
            new = advance(here, flux, flux_next, left[0], mean_next)
            for k, value in zip(order, new):
                cells[k, level] = value
                if sub == SUB - 1:
                    store = pltpu.make_async_copy(cells.at[k, level], outs[k].at[0, level], out_sem.at[k, level])
                    store.start()
                    stores.append(store)
    for store in stores:
        store.wait()


def on_device(*args):
    hbm = pl.BlockSpec(memory_space=pl.ANY)
    local = pl.BlockSpec(memory_space=pltpu.VMEM)
    dma, regular = pltpu.SemaphoreType.DMA, pltpu.SemaphoreType.REGULAR

    def vmem(*dims):
        return pltpu.VMEM(dims, jnp.float32)

    held = pl.pallas_call(
        exchange_kernel,
        out_shape=(vmem(3, LEVELS, ROWS, LONS), vmem(2, CHIPS, ROWS, HALF), vmem(2, 5, ROWS, LONS)),
        in_specs=[hbm] * 10,
        out_specs=(local,) * 3,
        scratch_shapes=[
            vmem(LEVELS - 1, ROWS, LONS),
            vmem(ROWS, LONS),
            pltpu.VMEM((ROWS, LONS), jnp.int32),
            pltpu.SMEM((1, REGIONS), jnp.float32),
            pltpu.SMEM((1,), jnp.int32),
            vmem(2, MEMBERS, ROWS, HALF),
            vmem(2, 5, ROWS, LONS),
            dma((8,)), dma((2,)), dma, dma((2,)), dma, dma((2,)), dma((3, 2)), dma((3, 2)), regular, regular,
        ],
        compiler_params=pltpu.CompilerParams(collective_id=0, has_side_effects=True),
    )(*args)
    held = [pltpu.with_memory_space_constraint(x, pltpu.VMEM) for x in held]
    return pl.pallas_call(
        finish_kernel,
        out_shape=(jax.ShapeDtypeStruct(args[0].shape, jnp.float32),) * 3,
        in_specs=[local] * 3,
        out_specs=(hbm,) * 3,
        scratch_shapes=[
            vmem(3, LEVELS, ROWS, LONS), vmem(4, ROWS, LONS), vmem(3, ROWS, LONS), vmem(3, ROWS, LONS),
            vmem(ROWS, LONS), dma((3, LEVELS)),
        ],
    )(*held)


def solution(mesh):
    moments = P("member", None, "band", None)
    return jax.shard_map(
        on_device,
        mesh=mesh,
        in_specs=(
            moments, moments, moments, moments, moments,
            P(None, "band", None),
            P("band", None),
            P("band", None),
            P("member", None),
            P("band"),
        ),
        out_specs=(moments,) * 3,
        check_vma=False,
    )
```

time: 33.2 us -> 28.3 us (0.85)
  the two profiles are of different devices: /device:TPU:384 before, /device:TPU:226 now
where the time goes in v2:
time: 28.3 us; the launch traced here: 28.1 us
  Pallas kernels  26.8 us (95%)
  between operations  1.29 us (5%)
    pallas_call x1, Pallas kernels, on_device(): pl.pallas_call(exchange_kernel, out_shape=(vmem(3, LEVELS, ROWS, LONS), v...  25.2 us
    pallas_call x1, Pallas kernels, on_device(): pl.pallas_call(finish_kernel, out_shape=(jax.ShapeDtypeStruct(args[0].sha...  1.64 us

profile of v2, /device:TPU:226, one launch (start us, length us, event | category | flops | bytes accessed | tf_op | source)
XLA Modules:
  0.0 28.1 jit_solution(11089200430411834131)
XLA Ops:
  1.3 25.2 %shard_map.121 = (f32[3,4,8,768]{3,2,1,0:T(8,128)S(1)}, f32[2,8,8,384]{3,2,1,0:T(8,128)S(1)}, f32[2,5,8,768]{3,2,1,0:T(8,128)S(1)}) custom-call(f32[1,4,8,768]{3,2,1,0:T(8,128)} %mean_h.1, f32[1,4,8,768]{3,2,1,0:T(8,128)} %lon_h.1, f32[1,4,8,768]{3,2,1,0:T(8,128)} %lat_h.1, f32[1,4,8,768]{3,2,1,0:T(8,128)} %zon_h.1, f32[1,4,8,768]{3,2,1,0:T(8,128)} %mer_h.1, ...), custom_call_target="tpu_custom_call" | custom-call | tf_op jit(solution)/shard_map/pallas_call | solution.py:356
  26.5 1.6 %shard_map.122 = (f32[1,4,8,768]{3,2,1,0:T(8,128)}, f32[1,4,8,768]{3,2,1,0:T(8,128)}, f32[1,4,8,768]{3,2,1,0:T(8,128)}) custom-call(f32[3,4,8,768]{3,2,1,0:T(8,128)S(1)} %get-tuple-element.6.cells_in, f32[2,8,8,384]{3,2,1,0:T(8,128)S(1)} %get-tuple-element.7.winds, f32[2,5,8,768]{3,2,1,0:T(8,128)S(1)} %get-tuple-element.8.halo), custom_call_target="tpu_custom_call" | custom-call | tf_op jit(solution)/shard_map/pallas_call | solution.py:374

commit v3 on v2

--- a/solution.py
+++ b/solution.py
@@ -8,9 +8,8 @@
 SUB = 2
 MESH = pl.DeviceIdType.MESH
 LEVELS, ROWS, LONS, REGIONS = 4, 8, 768, 22
-MEMBERS, CHIPS, HALF = 16, 8, 384
+MEMBERS, LINE = 16, 8
 U, V = 3, 4
-OFFSETS = ((2, 1), (1, 1), (3, 1), (2, 0), (0, 1), (1, 0), (3, 0), (0, 0))
 
 
 def upwind(faces, left, right):
@@ -37,24 +36,27 @@
     return advance(cells, flux, flux_next, left[0], pltpu.roll(cells[0], count - 1, 1))
 
 
-def wind_of(winds, c, level):
-    return jnp.concatenate([winds[c, 2 * level], winds[c, 2 * level + 1]], -1)
-
-
 def exchange_kernel(
     mean_h, lon_h, lat_h, zon_h, mer_h, mix_h, flux_h, region_h, scaling_h, reader_h,
     cells, winds, halo,
-    mix_v, flux_v, region_v, scaling_s, reader_s, got, pack,
-    in_sem, own_sem, scatter_send, scatter_recv, gather_send, gather_recv,
+    mix_v, flux_v, region_v, scaling_s, reader_s, got, tail, mine, theirs, pack,
+    in_sem, own_sem, scatter_send, scatter_recv, tail_recv, swap_send, swap_recv, gather_send, gather_recv,
     halo_send, halo_recv, late, beside,
 ):
     band, me = lax.axis_index("band"), lax.axis_index("member")
     bands = lax.axis_size("band")
-    chip, core = me // 2, me % 2
+    row, line, core = me // 4, (me // 2) % 2, me % 2
+    place = 2 * row + core
     has_south, has_north = band > 0, band < bands - 1
     around = has_south.astype(jnp.int32) + has_north.astype(jnp.int32)
     tail_end = me == 0
     answers = jnp.logical_and(tail_end, band % 2 == 0)
+    owns = place != 0
+    owns_spare = place == 1
+    partner = me + 2 - 4 * line
+
+    def member(where, which):
+        return (where // 2 * 2 + which) * 2 + where % 2
 
     loads = [
         pltpu.make_async_copy(mix_h, mix_v, in_sem.at[3]),
@@ -73,50 +75,76 @@
             def _():
                 pl.semaphore_signal(semaphore, inc=1, device_id=(band + step, me), device_id_type=MESH)
 
-    def signal_members(semaphore):
-        for step in range(1, MEMBERS):
-            pl.semaphore_signal(semaphore, inc=1, device_id=(band, (me + step) % MEMBERS), device_id_type=MESH)
+    def signal_line(semaphore, which, first):
+        for step in range(first, LINE):
+            target = member((place + step) % LINE, which)
+            pl.semaphore_signal(semaphore, inc=1, device_id=(band, target), device_id_type=MESH)
 
     barrier = pltpu.get_barrier_semaphore()
-    pl.when(jnp.logical_not(tail_end))(lambda: signal_members(barrier))
+
+    @pl.when(jnp.logical_not(tail_end))
+    def _():
+        signal_line(barrier, line, 1)
+
+        @pl.when(line == 1)
+        def _():
+            pl.semaphore_signal(barrier, inc=1, device_id=(band, 0), device_id_type=MESH)
+
+        @pl.when(owns)
+        def _():
+            pl.semaphore_signal(barrier, inc=1, device_id=(band, partner), device_id_type=MESH)
+
     pl.when(jnp.logical_not(answers))(lambda: signal_beside(barrier))
+    others = jnp.where(jnp.logical_and(line == 1, owns), LINE, LINE - 1)
     pl.semaphore_wait(
         barrier,
-        jnp.where(tail_end, jnp.where(answers, MEMBERS - 1 + around, MEMBERS - 1), MEMBERS - 2 + around),
+        jnp.where(tail_end, jnp.where(answers, MEMBERS - 1 + around, MEMBERS - 1), others + around),
     )
 
-    def piece(c, q):
-        source = mer_h if c else zon_h
-        return source.at[0, q // 2, :, pl.ds(pl.multiple_of((q % 2) * HALF, HALF), HALF)]
-
-    for dy, dx in OFFSETS:
-        q = ((chip // 2 + dy) % 4) * 2 + (chip + dx) % 2
-        for c in range(2):
-            owner = jnp.maximum(2 * q + c, 1)
-            spare = (owner != 2 * q + c).astype(jnp.int32)
-
-            def send():
-                pltpu.make_async_remote_copy(
-                    src_ref=piece(c, q), dst_ref=got.at[spare, me], send_sem=scatter_send,
-                    recv_sem=scatter_recv.at[spare], device_id=(band, owner), device_id_type=MESH,
-                ).start()
-
-            def keep():
-                pltpu.make_async_copy(piece(c, q), got.at[spare, me], own_sem.at[spare]).start()
-
-            if (dy, dx) == (0, 0):
-                pl.when(owner != me)(send)
-                pl.when(owner == me)(keep)
-            else:
-                send()
+    def piece(c, level):
+        return (mer_h if c else zon_h).at[0, level]
+
+    def target_of(c, level, which):
+        spare = jnp.where(level == 0, 1 - c, 0)
+        return spare, member(2 * level + jnp.maximum(c, spare), which)
+
+    @pl.when(tail_end)
+    def _():
+        for which in (1, 0):
+            for level in (2, 1, 3, 0):
+                for c in range(2):
+                    spare, owner = target_of(c, level, which)
+                    pltpu.make_async_remote_copy(
+                        src_ref=piece(c, level), dst_ref=tail.at[spare], send_sem=scatter_send,
+                        recv_sem=tail_recv.at[spare], device_id=(band, owner), device_id_type=MESH,
+                    ).start()
+        signal_line(late, 0, 1)
+
+    @pl.when(jnp.logical_not(tail_end))
+    def _():
+        for step in (2, 1, 3, 0):
+            level = (row + step) % LEVELS
+            for c in range(2):
+                spare, owner = target_of(c, level, line)
+
+                def send():
+                    pltpu.make_async_remote_copy(
+                        src_ref=piece(c, level), dst_ref=got.at[spare, place], send_sem=scatter_send,
+                        recv_sem=scatter_recv.at[spare], device_id=(band, owner), device_id_type=MESH,
+                    ).start()
+
+                def keep():
+                    pltpu.make_async_copy(piece(c, level), got.at[spare, place], own_sem.at[spare]).start()
+
+                if step:
+                    send()
+                else:
+                    pl.when(owner != me)(send)
+                    pl.when(owner == me)(keep)
 
     load_reader.start()
     for load in loads:
         load.start()
-
-    @pl.when(tail_end)
-    def _():
-        signal_members(late)
 
     pl.when(answers)(lambda: signal_beside(beside))
 
@@ -179,47 +207,70 @@
 
     send_across(0)
 
-    most = got.at[0, pl.ds(0, MEMBERS - 1)]
-
     def arrive(spare):
-        kept = got.at[spare, me]
+        kept = got.at[spare, place]
         pltpu.make_async_copy(kept, kept, own_sem.at[spare]).wait()
-        pltpu.make_async_copy(most, most, scatter_recv.at[spare]).wait()
-
-    def pass_on(c, q, target):
+        for count in (LINE - 2, LINE - 1):
+            @pl.when(line == count - (LINE - 2))
+            def _():
+                part = got.at[spare, pl.ds(0, count)]
+                pltpu.make_async_copy(part, part, scatter_recv.at[spare]).wait()
+
+    reader = reader_s[0]
+    reader_line = (reader // 2) % 2
+    reader_place = jnp.maximum(reader // 4 * 2 + reader % 2, 1 - line)
+
+    def swap(spare):
+        return pltpu.make_async_remote_copy(
+            src_ref=mine.at[spare], dst_ref=theirs.at[spare], send_sem=swap_send.at[spare],
+            recv_sem=swap_recv.at[spare], device_id=(band, partner), device_id_type=MESH,
+        )
+
+    def offer(spare):
+        mine[spare] = got[spare, reader_place]
+        swap(spare).start()
+
+    def settle(spare, c, level):
+        swap(spare).wait_recv()
+        pltpu.make_async_copy(tail.at[spare], tail.at[spare], tail_recv.at[spare]).wait()
+        winds[c, level] = jnp.where(
+            reader == 0, tail[spare], jnp.where(reader_line == line, mine[spare], theirs[spare])
+        )
+
+    def pass_on(c, level, target):
         pltpu.make_async_remote_copy(
-            src_ref=winds.at[c, q], dst_ref=winds.at[c, q], send_sem=gather_send,
+            src_ref=winds.at[c, level], dst_ref=winds.at[c, level], send_sem=gather_send,
             recv_sem=gather_recv.at[c], device_id=(band, target), device_id_type=MESH,
         ).start()
 
-    @pl.when(jnp.logical_not(tail_end))
+    def share(c, level):
+        for step in (4, 5, 3, 2, 6, 7, 1):
+            target = member((place + step) % LINE, line)
+            pl.when(target != 0)(lambda: pass_on(c, level, target))
+
+    @pl.when(owns)
     def _():
         arrive(0)
-        pl.when(me == 1)(lambda: arrive(1))
-        winds[core, chip] = got[0, reader_s[0]]
-        for dy, dx in OFFSETS:
-            q = ((chip // 2 + dy) % 4) * 2 + (chip + dx) % 2
-            for c in range(2):
-                target = 2 * q + c
-
-                @pl.when(jnp.logical_and(target != me, target != 0))
-                def _():
-                    pass_on(core, chip, target)
-
-        pl.semaphore_wait(late, 1)
-        pass_on(core, chip, 0)
-
-    @pl.when(me == 1)
-    def _():
-        winds[0, 0] = got[1, reader_s[0]]
-        for target in [*range(MEMBERS - 1, 1, -1), 0]:
-            pass_on(0, 0, target)
+        pl.when(owns_spare)(lambda: arrive(1))
+        offer(0)
+        pl.when(owns_spare)(lambda: offer(1))
+        settle(0, core, row)
+        share(core, row)
+
+        @pl.when(owns_spare)
+        def _():
+            settle(1, 0, 0)
+            share(0, 0)
+
+        @pl.when(line == 0)
+        def _():
+            pl.semaphore_wait(late, 1)
+            pass_on(core, row, 0)
+            pl.when(owns_spare)(lambda: pass_on(0, 0, 0))
 
     def await_winds(c):
-        mine = jnp.logical_and(jnp.logical_not(tail_end), core == c)
-        if c == 0:
-            mine = jnp.logical_or(mine, me == 1)
-        for count, case in ((CHIPS - 1, mine), (CHIPS, jnp.logical_not(mine))):
+        mine_too = jnp.logical_and(owns, jnp.logical_or(core == c, owns_spare))
+        for count, case in ((LEVELS - 1, mine_too), (LEVELS, jnp.logical_not(mine_too))):
             @pl.when(case)
             def _():
                 part = winds.at[c, pl.ds(0, count)]
@@ -228,13 +279,13 @@
     for c in range(2):
         await_winds(c)
         for level in range(LEVELS):
-            rows = wind_of(winds, c, level)
+            rows = winds[c, level]
             pack[0, U + c, pl.ds(2 * level, 2), :] = rows[:2]
             pack[1, U + c, pl.ds(2 * level, 2), :] = rows[ROWS - 2:]
         send_across(1 + c)
 
     for level in range(LEVELS):
-        new = zonal((cells[0, level], cells[1, level], cells[2, level]), wind_of(winds, 0, level))
+        new = zonal((cells[0, level], cells[1, level], cells[2, level]), winds[0, level])
         for k in range(3):
             cells[k, level] = new[k]
 
@@ -243,26 +294,29 @@
         def _():
             halo[side] = jnp.zeros((5, ROWS, LONS), jnp.float32)
 
+    def drain(count, semaphore):
+        part = got.at[0, pl.ds(0, count)]
+        pltpu.make_async_copy(part, part, semaphore).wait()
+
     @pl.when(tail_end)
     def _():
-        every = got.at[0]
-        pltpu.make_async_copy(every, every, scatter_send).wait()
-
-    @pl.when(jnp.logical_not(tail_end))
-    def _():
-        sent = got.at[0, pl.ds(0, MEMBERS - 1)]
-
-        @pl.when(me == 1)
-        def _():
-            some = got.at[0, pl.ds(0, MEMBERS - 2)]
-            pltpu.make_async_copy(some, some, scatter_send).wait()
-            pltpu.make_async_copy(sent, sent, gather_send).wait()
-
-        @pl.when(me != 1)
-        def _():
-            pltpu.make_async_copy(sent, sent, scatter_send).wait()
-
-        pltpu.make_async_copy(sent, sent, gather_send).wait()
+        drain(LINE, scatter_send)
+        drain(LINE, scatter_send)
+
+    pl.when(me == 2)(lambda: drain(LINE, scatter_send))
+
+    @pl.when(owns)
+    def _():
+        drain(LINE - 2, scatter_send)
+        swap(0).wait_send()
+        drain(LINE - 1, gather_send)
+
+        @pl.when(owns_spare)
+        def _():
+            swap(1).wait_send()
+            drain(LINE - 1, gather_send)
+
+        pl.when(jnp.logical_not(owns_spare))(lambda: drain(1, scatter_send))
 
     for part in range(3):
         for side, there in sides:
@@ -293,7 +347,7 @@
     n_cells = tuple(halo[1, k] for k in range(3))
     v_north = jnp.where(last_band, 0.0, halo[1, V])
     for level in range(LEVELS):
-        edge[3, pl.ds(2 * level + 1, 1), :] = wind_of(winds, 1, level)[:1]
+        edge[3, pl.ds(2 * level + 1, 1), :] = winds[1, level][:1]
         edge[3, pl.ds(2 * level, 1), :] = jnp.zeros((1, LONS), jnp.float32)
     stores = []
     for sub in range(SUB):
@@ -301,7 +355,7 @@
         for level in range(LEVELS):
             here = tuple(source[k, level] for k in range(3))
             if sub:
-                here = zonal(here, wind_of(winds, 0, level))
+                here = zonal(here, winds[0, level])
             for k in range(3):
                 if sub:
                     cells[k, level] = here[k]
@@ -324,7 +378,7 @@
             n_cells = meridional(advance(n_mer, flux_8, flux_9, e_mer[0], down(n_mer[0])))
         source = cells if sub else cells_in
         for level in range(LEVELS):
-            faces = jnp.where(jnp.logical_and(row == 0, first_band), 0.0, wind_of(winds, 1, level))
+            faces = jnp.where(jnp.logical_and(row == 0, first_band), 0.0, winds[1, level])
             here = tuple(source[k, level] for k in order)
             left = tuple(
                 jnp.where(row == 0, south[k, pl.ds(2 * level + 1, 1), :], up(x)) for k, x in enumerate(here)
@@ -355,7 +409,7 @@
 
     held = pl.pallas_call(
         exchange_kernel,
-        out_shape=(vmem(3, LEVELS, ROWS, LONS), vmem(2, CHIPS, ROWS, HALF), vmem(2, 5, ROWS, LONS)),
+        out_shape=(vmem(3, LEVELS, ROWS, LONS), vmem(2, LEVELS, ROWS, LONS), vmem(2, 5, ROWS, LONS)),
         in_specs=[hbm] * 10,
         out_specs=(local,) * 3,
         scratch_shapes=[
@@ -364,9 +418,12 @@
             pltpu.VMEM((ROWS, LONS), jnp.int32),
             pltpu.SMEM((1, REGIONS), jnp.float32),
             pltpu.SMEM((1,), jnp.int32),
-            vmem(2, MEMBERS, ROWS, HALF),
+            vmem(2, LINE, ROWS, LONS),
+            vmem(2, ROWS, LONS),
+            vmem(2, ROWS, LONS),
+            vmem(2, ROWS, LONS),
             vmem(2, 5, ROWS, LONS),
-            dma((8,)), dma((2,)), dma, dma((2,)), dma, dma((2,)), dma((3, 2)), dma((3, 2)), regular, regular,
+            dma((8,)), dma((2,)), dma, dma((2,)), dma((2,)), dma((2,)), dma((2,)), dma, dma((2,)), dma((3, 2)), dma((3, 2)), regular, regular,
         ],
         compiler_params=pltpu.CompilerParams(collective_id=0, has_side_effects=True),
     )(*args)

time: 28.3 us -> 26 us (0.919)
  Pallas kernels: 26.8 us -> 24.5 us
    pallas_call x1, Pallas kernels: 25.2 us -> 22.9 us  [on_device(): pl.pallas_call(exchange_kernel, out_shape=(vmem(3, LEVELS, ROWS, LONS), v...]
where the time goes in v3:
time: 26 us; the launch traced here: 25.8 us
  Pallas kernels  24.5 us (94%)
  between operations  1.29 us (5%)
    pallas_call x1, Pallas kernels, on_device(): pl.pallas_call(exchange_kernel, out_shape=(vmem(3, LEVELS, ROWS, LONS), v...  22.9 us
    pallas_call x1, Pallas kernels, on_device(): pl.pallas_call(finish_kernel, out_shape=(jax.ShapeDtypeStruct(args[0].sha...  1.64 us

profile of v3, /device:TPU:226, one launch (start us, length us, event | category | flops | bytes accessed | tf_op | source)
XLA Modules:
  0.0 25.8 jit_solution(10657566815343854720)
XLA Ops:
  1.3 22.9 %shard_map.121 = (f32[3,4,8,768]{3,2,1,0:T(8,128)S(1)}, f32[2,4,8,768]{3,2,1,0:T(8,128)S(1)}, f32[2,5,8,768]{3,2,1,0:T(8,128)S(1)}) custom-call(f32[1,4,8,768]{3,2,1,0:T(8,128)} %mean_h.1, f32[1,4,8,768]{3,2,1,0:T(8,128)} %lon_h.1, f32[1,4,8,768]{3,2,1,0:T(8,128)} %lat_h.1, f32[1,4,8,768]{3,2,1,0:T(8,128)} %zon_h.1, f32[1,4,8,768]{3,2,1,0:T(8,128)} %mer_h.1, ...), custom_call_target="tpu_custom_call" | custom-call | tf_op jit(solution)/shard_map/pallas_call | solution.py:410
  24.2 1.6 %shard_map.122 = (f32[1,4,8,768]{3,2,1,0:T(8,128)}, f32[1,4,8,768]{3,2,1,0:T(8,128)}, f32[1,4,8,768]{3,2,1,0:T(8,128)}) custom-call(f32[3,4,8,768]{3,2,1,0:T(8,128)S(1)} %get-tuple-element.6.cells_in, f32[2,4,8,768]{3,2,1,0:T(8,128)S(1)} %get-tuple-element.7.winds, f32[2,5,8,768]{3,2,1,0:T(8,128)S(1)} %get-tuple-element.8.halo), custom_call_target="tpu_custom_call" | custom-call | tf_op jit(solution)/shard_map/pallas_call | solution.py:431

commit v4 on v3

--- a/solution.py
+++ b/solution.py
@@ -8,7 +8,7 @@
 SUB = 2
 MESH = pl.DeviceIdType.MESH
 LEVELS, ROWS, LONS, REGIONS = 4, 8, 768, 22
-MEMBERS, LINE = 16, 8
+LINE = 8
 U, V = 3, 4
 
 
@@ -39,8 +39,8 @@
 def exchange_kernel(
     mean_h, lon_h, lat_h, zon_h, mer_h, mix_h, flux_h, region_h, scaling_h, reader_h,
     cells, winds, halo,
-    mix_v, flux_v, region_v, scaling_s, reader_s, got, tail, mine, theirs, pack,
-    in_sem, own_sem, scatter_send, scatter_recv, tail_recv, swap_send, swap_recv, gather_send, gather_recv,
+    mix_v, flux_v, region_v, scaling_s, reader_s, got, mine, theirs, slips, slips_in, beyond, pack,
+    in_sem, own_sem, scatter_send, scatter_recv, swap_send, swap_recv, slip_send, slip_recv, gather_send, gather_recv,
     halo_send, halo_recv, late, beside,
 ):
     band, me = lax.axis_index("band"), lax.axis_index("member")
@@ -69,84 +69,67 @@
     ]
     load_reader = pltpu.make_async_copy(reader_h, reader_s, in_sem.at[7])
 
-    def signal_beside(semaphore):
+    def signal_beside(semaphore, who):
         for there, step in ((has_south, -1), (has_north, 1)):
             @pl.when(there)
             def _():
-                pl.semaphore_signal(semaphore, inc=1, device_id=(band + step, me), device_id_type=MESH)
-
-    def signal_line(semaphore, which, first):
-        for step in range(first, LINE):
-            target = member((place + step) % LINE, which)
+                pl.semaphore_signal(semaphore, inc=1, device_id=(band + step, who), device_id_type=MESH)
+
+    def signal_line(semaphore):
+        for step in range(1, LINE):
+            target = member((place + step) % LINE, line)
             pl.semaphore_signal(semaphore, inc=1, device_id=(band, target), device_id_type=MESH)
 
     barrier = pltpu.get_barrier_semaphore()
 
     @pl.when(jnp.logical_not(tail_end))
     def _():
-        signal_line(barrier, line, 1)
-
-        @pl.when(line == 1)
-        def _():
-            pl.semaphore_signal(barrier, inc=1, device_id=(band, 0), device_id_type=MESH)
-
-        @pl.when(owns)
-        def _():
-            pl.semaphore_signal(barrier, inc=1, device_id=(band, partner), device_id_type=MESH)
-
-    pl.when(jnp.logical_not(answers))(lambda: signal_beside(barrier))
-    others = jnp.where(jnp.logical_and(line == 1, owns), LINE, LINE - 1)
-    pl.semaphore_wait(
-        barrier,
-        jnp.where(tail_end, jnp.where(answers, MEMBERS - 1 + around, MEMBERS - 1), others + around),
-    )
+        signal_line(barrier)
+
+    @pl.when(owns)
+    def _():
+        pl.semaphore_signal(barrier, inc=1, device_id=(band, partner), device_id_type=MESH)
+        signal_beside(barrier, partner)
+
+    pl.when(jnp.logical_not(answers))(lambda: signal_beside(barrier, me))
+    in_line = jnp.where(jnp.logical_and(line == 0, owns), LINE - 2, LINE - 1)
+    outside = jnp.where(owns, 1 + 2 * around, jnp.where(jnp.logical_or(answers, me == 2), around, 0))
+    pl.semaphore_wait(barrier, in_line + outside)
 
     def piece(c, level):
         return (mer_h if c else zon_h).at[0, level]
 
-    def target_of(c, level, which):
+    def target_of(c, level):
         spare = jnp.where(level == 0, 1 - c, 0)
-        return spare, member(2 * level + jnp.maximum(c, spare), which)
-
-    @pl.when(tail_end)
-    def _():
-        for which in (1, 0):
-            for level in (2, 1, 3, 0):
-                for c in range(2):
-                    spare, owner = target_of(c, level, which)
-                    pltpu.make_async_remote_copy(
-                        src_ref=piece(c, level), dst_ref=tail.at[spare], send_sem=scatter_send,
-                        recv_sem=tail_recv.at[spare], device_id=(band, owner), device_id_type=MESH,
-                    ).start()
-        signal_line(late, 0, 1)
-
-    @pl.when(jnp.logical_not(tail_end))
-    def _():
-        for step in (2, 1, 3, 0):
-            level = (row + step) % LEVELS
-            for c in range(2):
-                spare, owner = target_of(c, level, line)
-
-                def send():
-                    pltpu.make_async_remote_copy(
-                        src_ref=piece(c, level), dst_ref=got.at[spare, place], send_sem=scatter_send,
-                        recv_sem=scatter_recv.at[spare], device_id=(band, owner), device_id_type=MESH,
-                    ).start()
-
-                def keep():
-                    pltpu.make_async_copy(piece(c, level), got.at[spare, place], own_sem.at[spare]).start()
-
-                if step:
-                    send()
-                else:
-                    pl.when(owner != me)(send)
-                    pl.when(owner == me)(keep)
+        return spare, member(2 * level + jnp.maximum(c, spare), line)
+
+    for step in (2, 1, 3, 0):
+        level = (row + step) % LEVELS
+        for c in range(2):
+            spare, owner = target_of(c, level)
+
+            def send():
+                pltpu.make_async_remote_copy(
+                    src_ref=piece(c, level), dst_ref=got.at[spare, place], send_sem=scatter_send,
+                    recv_sem=scatter_recv.at[spare], device_id=(band, owner), device_id_type=MESH,
+                ).start()
+
+            def keep():
+                pltpu.make_async_copy(piece(c, level), got.at[spare, place], own_sem.at[spare]).start()
+
+            if step:
+                send()
+            else:
+                pl.when(owner != me)(send)
+                pl.when(owner == me)(keep)
+
+    pl.when(tail_end)(lambda: signal_line(late))
 
     load_reader.start()
     for load in loads:
         load.start()
 
-    pl.when(answers)(lambda: signal_beside(beside))
+    pl.when(answers)(lambda: signal_beside(beside, me))
 
     for load in loads[:4]:
         load.wait()
@@ -185,19 +168,14 @@
             pack[0, k, pl.ds(2 * level, 2), :] = result[:2]
             pack[1, k, pl.ds(2 * level, 2), :] = result[ROWS - 2:]
 
-    def across(side, part, first, count):
+    def across(side):
         return pltpu.make_async_remote_copy(
-            src_ref=pack.at[side, pl.ds(first, count)], dst_ref=halo.at[1 - side, pl.ds(first, count)],
-            send_sem=halo_send.at[part, side], recv_sem=halo_recv.at[part, 1 - side],
+            src_ref=pack.at[side], dst_ref=halo.at[1 - side, pl.ds(0, 3)],
+            send_sem=halo_send.at[side], recv_sem=halo_recv.at[1 - side],
             device_id=(band + (1 if side else -1), me), device_id_type=MESH,
         )
 
-    parts = ((0, 3), (U, 1), (V, 1))
     sides = ((0, has_south), (1, has_north))
-
-    def send_across(part):
-        for side, there in sides:
-            pl.when(there)(across(side, part, *parts[part]).start)
 
     load_reader.wait()
 
@@ -205,20 +183,18 @@
     def _():
         pl.semaphore_wait(beside, around)
 
-    send_across(0)
+    for side, there in sides:
+        pl.when(there)(across(side).start)
 
     def arrive(spare):
         kept = got.at[spare, place]
         pltpu.make_async_copy(kept, kept, own_sem.at[spare]).wait()
-        for count in (LINE - 2, LINE - 1):
-            @pl.when(line == count - (LINE - 2))
-            def _():
-                part = got.at[spare, pl.ds(0, count)]
-                pltpu.make_async_copy(part, part, scatter_recv.at[spare]).wait()
+        part = got.at[spare, pl.ds(0, LINE - 1)]
+        pltpu.make_async_copy(part, part, scatter_recv.at[spare]).wait()
 
     reader = reader_s[0]
-    reader_line = (reader // 2) % 2
-    reader_place = jnp.maximum(reader // 4 * 2 + reader % 2, 1 - line)
+    here = (reader // 2) % 2 == line
+    reader_place = reader // 4 * 2 + reader % 2
 
     def swap(spare):
         return pltpu.make_async_remote_copy(
@@ -226,27 +202,49 @@
             recv_sem=swap_recv.at[spare], device_id=(band, partner), device_id_type=MESH,
         )
 
+    def slip(spare, side, other):
+        return pltpu.make_async_remote_copy(
+            src_ref=slips.at[spare, side], dst_ref=slips_in.at[spare, 1 - side, other],
+            send_sem=slip_send.at[spare, side, other], recv_sem=slip_recv.at[spare, 1 - side, other],
+            device_id=(band + (1 if side else -1), partner if other else me), device_id_type=MESH,
+        )
+
     def offer(spare):
-        mine[spare] = got[spare, reader_place]
+        chosen = got[spare, reader_place]
+        mine[spare] = chosen
         swap(spare).start()
+        slips[spare, 0] = jnp.where(here, chosen[:2], 0.0)
+        slips[spare, 1] = jnp.where(here, chosen[ROWS - 2:], 0.0)
+        for side, there in sides:
+            for other in (1, 0):
+                pl.when(there)(slip(spare, side, other).start)
 
     def settle(spare, c, level):
         swap(spare).wait_recv()
-        pltpu.make_async_copy(tail.at[spare], tail.at[spare], tail_recv.at[spare]).wait()
-        winds[c, level] = jnp.where(
-            reader == 0, tail[spare], jnp.where(reader_line == line, mine[spare], theirs[spare])
-        )
-
-    def pass_on(c, level, target):
+        winds[c, level] = jnp.where(here, mine[spare], theirs[spare])
+
+    def settle_beside(spare, c, level):
+        for side, there in sides:
+            @pl.when(there)
+            def _():
+                for other in range(2):
+                    slip(spare, 1 - side, other).wait_recv()
+                beyond[c, level, pl.ds(2 * side, 2), :] = slips_in[spare, side, 0] + slips_in[spare, side, 1]
+
+            @pl.when(jnp.logical_not(there))
+            def _():
+                beyond[c, level, pl.ds(2 * side, 2), :] = jnp.zeros((2, LONS), jnp.float32)
+
+    def pass_on(ref, part, c, level, target):
         pltpu.make_async_remote_copy(
-            src_ref=winds.at[c, level], dst_ref=winds.at[c, level], send_sem=gather_send,
-            recv_sem=gather_recv.at[c], device_id=(band, target), device_id_type=MESH,
+            src_ref=ref.at[c, level], dst_ref=ref.at[c, level], send_sem=gather_send.at[part],
+            recv_sem=gather_recv.at[part, c], device_id=(band, target), device_id_type=MESH,
         ).start()
 
-    def share(c, level):
+    def share(ref, part, c, level):
         for step in (4, 5, 3, 2, 6, 7, 1):
             target = member((place + step) % LINE, line)
-            pl.when(target != 0)(lambda: pass_on(c, level, target))
+            pl.when(target != 0)(lambda: pass_on(ref, part, c, level, target))
 
     @pl.when(owns)
     def _():
@@ -255,75 +253,80 @@
         offer(0)
         pl.when(owns_spare)(lambda: offer(1))
         settle(0, core, row)
-        share(core, row)
+        share(winds, 0, core, row)
 
         @pl.when(owns_spare)
         def _():
             settle(1, 0, 0)
-            share(0, 0)
+            share(winds, 0, 0, 0)
+
+        settle_beside(0, core, row)
+        share(beyond, 1, core, row)
+
+        @pl.when(owns_spare)
+        def _():
+            settle_beside(1, 0, 0)
+            share(beyond, 1, 0, 0)
 
         @pl.when(line == 0)
         def _():
             pl.semaphore_wait(late, 1)
-            pass_on(core, row, 0)
-            pl.when(owns_spare)(lambda: pass_on(0, 0, 0))
-
-    def await_winds(c):
+            for part, ref in enumerate((winds, beyond)):
+                pass_on(ref, part, core, row, 0)
+                pl.when(owns_spare)(lambda: pass_on(ref, part, 0, 0, 0))
+
+    def await_winds(ref, part, c):
         mine_too = jnp.logical_and(owns, jnp.logical_or(core == c, owns_spare))
         for count, case in ((LEVELS - 1, mine_too), (LEVELS, jnp.logical_not(mine_too))):
             @pl.when(case)
             def _():
-                part = winds.at[c, pl.ds(0, count)]
-                pltpu.make_async_copy(part, part, gather_recv.at[c]).wait()
-
-    for c in range(2):
-        await_winds(c)
-        for level in range(LEVELS):
-            rows = winds[c, level]
-            pack[0, U + c, pl.ds(2 * level, 2), :] = rows[:2]
-            pack[1, U + c, pl.ds(2 * level, 2), :] = rows[ROWS - 2:]
-        send_across(1 + c)
-
+                some = ref.at[c, pl.ds(0, count)]
+                pltpu.make_async_copy(some, some, gather_recv.at[part, c]).wait()
+
+    await_winds(winds, 0, 0)
     for level in range(LEVELS):
         new = zonal((cells[0, level], cells[1, level], cells[2, level]), winds[0, level])
         for k in range(3):
             cells[k, level] = new[k]
 
+    await_winds(winds, 0, 1)
+    for c in range(2):
+        await_winds(beyond, 1, c)
+        for level in range(LEVELS):
+            for side in range(2):
+                halo[side, U + c, pl.ds(2 * level, 2), :] = beyond[c, level, pl.ds(2 * side, 2), :]
+
+    def drain(ref, count, semaphore):
+        some = ref.at[0, pl.ds(0, count)]
+        pltpu.make_async_copy(some, some, semaphore).wait()
+
+    def drain_owner(spare):
+        swap(spare).wait_send()
+        for side, there in sides:
+            for other in range(2):
+                pl.when(there)(slip(spare, side, other).wait_send)
+        for part, ref in enumerate((winds, beyond)):
+            drain(ref, LEVELS, gather_send.at[part])
+            drain(ref, LEVELS - 1, gather_send.at[part])
+
+    drain(got, LINE - 2, scatter_send)
+    pl.when(jnp.logical_not(owns))(lambda: drain(got, 2, scatter_send))
+
+    @pl.when(owns)
+    def _():
+        drain_owner(0)
+        pl.when(owns_spare)(lambda: drain_owner(1))
+        pl.when(jnp.logical_not(owns_spare))(lambda: drain(got, 1, scatter_send))
+
     for side, there in sides:
+        @pl.when(there)
+        def _():
+            across(side).wait_send()
+            across(1 - side).wait_recv()
+
         @pl.when(jnp.logical_not(there))
         def _():
-            halo[side] = jnp.zeros((5, ROWS, LONS), jnp.float32)
-
-    def drain(count, semaphore):
-        part = got.at[0, pl.ds(0, count)]
-        pltpu.make_async_copy(part, part, semaphore).wait()
-
-    @pl.when(tail_end)
-    def _():
-        drain(LINE, scatter_send)
-        drain(LINE, scatter_send)
-
-    pl.when(me == 2)(lambda: drain(LINE, scatter_send))
-
-    @pl.when(owns)
-    def _():
-        drain(LINE - 2, scatter_send)
-        swap(0).wait_send()
-        drain(LINE - 1, gather_send)
-
-        @pl.when(owns_spare)
-        def _():
-            swap(1).wait_send()
-            drain(LINE - 1, gather_send)
-
-        pl.when(jnp.logical_not(owns_spare))(lambda: drain(1, scatter_send))
-
-    for part in range(3):
-        for side, there in sides:
-            @pl.when(there)
-            def _():
-                across(side, part, *parts[part]).wait_send()
-                across(1 - side, part, *parts[part]).wait_recv()
+            halo[side, pl.ds(0, 3)] = jnp.zeros((3, ROWS, LONS), jnp.float32)
 
 
 def finish_kernel(cells_in, winds, halo, out_mean, out_lon, out_lat, cells, edge, south, last, north, out_sem):
@@ -421,9 +424,12 @@
             vmem(2, LINE, ROWS, LONS),
             vmem(2, ROWS, LONS),
             vmem(2, ROWS, LONS),
-            vmem(2, ROWS, LONS),
-            vmem(2, 5, ROWS, LONS),
-            dma((8,)), dma((2,)), dma, dma((2,)), dma((2,)), dma((2,)), dma((2,)), dma, dma((2,)), dma((3, 2)), dma((3, 2)), regular, regular,
+            vmem(2, 2, 2, LONS),
+            vmem(2, 2, 2, 2, LONS),
+            vmem(2, LEVELS, 4, LONS),
+            vmem(2, 3, ROWS, LONS),
+            dma((8,)), dma((2,)), dma, dma((2,)), dma((2,)), dma((2,)), dma((2, 2, 2)), dma((2, 2, 2)), dma((2,)), dma((2, 2)),
+            dma((2,)), dma((2,)), regular, regular,
         ],
         compiler_params=pltpu.CompilerParams(collective_id=0, has_side_effects=True),
     )(*args)

time: 26 us -> 23.2 us (0.89)
  the two profiles are of different devices: /device:TPU:226 before, /device:TPU:384 now
where the time goes in v4:
time: 23.2 us; the launch traced here: 23 us
  Pallas kernels  21.7 us (94%)
  between operations  1.29 us (6%)
    pallas_call x1, Pallas kernels, on_device(): pl.pallas_call(exchange_kernel, out_shape=(vmem(3, LEVELS, ROWS, LONS), v...  20.1 us
    pallas_call x1, Pallas kernels, on_device(): pl.pallas_call(finish_kernel, out_shape=(jax.ShapeDtypeStruct(args[0].sha...  1.64 us

profile of v4, /device:TPU:384, one launch (start us, length us, event | category | flops | bytes accessed | tf_op | source)
XLA Modules:
  0.0 23.0 jit_solution(9900451823269416073)
XLA Ops:
  1.3 20.1 %shard_map.121 = (f32[3,4,8,768]{3,2,1,0:T(8,128)S(1)}, f32[2,4,8,768]{3,2,1,0:T(8,128)S(1)}, f32[2,5,8,768]{3,2,1,0:T(8,128)S(1)}) custom-call(f32[1,4,8,768]{3,2,1,0:T(8,128)} %mean_h.1, f32[1,4,8,768]{3,2,1,0:T(8,128)} %lon_h.1, f32[1,4,8,768]{3,2,1,0:T(8,128)} %lat_h.1, f32[1,4,8,768]{3,2,1,0:T(8,128)} %zon_h.1, f32[1,4,8,768]{3,2,1,0:T(8,128)} %mer_h.1, ...), custom_call_target="tpu_custom_call" | custom-call | tf_op jit(solution)/shard_map/pallas_call | solution.py:413
  21.4 1.6 %shard_map.122 = (f32[1,4,8,768]{3,2,1,0:T(8,128)}, f32[1,4,8,768]{3,2,1,0:T(8,128)}, f32[1,4,8,768]{3,2,1,0:T(8,128)}) custom-call(f32[3,4,8,768]{3,2,1,0:T(8,128)S(1)} %get-tuple-element.6.cells_in, f32[2,4,8,768]{3,2,1,0:T(8,128)S(1)} %get-tuple-element.7.winds, f32[2,5,8,768]{3,2,1,0:T(8,128)S(1)} %get-tuple-element.8.halo), custom_call_target="tpu_custom_call" | custom-call | tf_op jit(solution)/shard_map/pallas_call | solution.py:437

commit v5 on v4

v5 whole, which is shorter than its diff:
```python
import jax
import jax.numpy as jnp
from jax import lax
from jax.experimental import pallas as pl
from jax.experimental.pallas import tpu as pltpu
from jax.sharding import PartitionSpec as P

SUB = 2
MESH = pl.DeviceIdType.MESH
LEVELS, ROWS, LONS, REGIONS = 4, 8, 768, 22
LINE, HALF = 8, 384


def upwind(faces, left, right):
    forward = faces > 0.0
    mean, along, cross = (jnp.where(forward, l, r) for l, r in zip(left, right))
    weight = 0.5 * (jnp.where(forward, 1.0, -1.0) - faces)
    return faces * (mean + weight * along), faces * along, faces * cross


def advance(cells, flux, flux_next, mean_prev, mean_next):
    mean, along, cross = cells
    return (
        mean + (flux[0] - flux_next[0]),
        0.5 * (along + (flux[1] - flux_next[1])) + 0.25 * (mean_next - mean_prev),
        cross + (flux[2] - flux_next[2]),
    )


def zonal(cells, faces):
    count = faces.shape[-1]
    left = tuple(pltpu.roll(x, 1, 1) for x in cells)
    flux = upwind(faces, left, cells)
    flux_next = tuple(pltpu.roll(x, count - 1, 1) for x in flux)
    return advance(cells, flux, flux_next, left[0], pltpu.roll(cells[0], count - 1, 1))


def wind_of(winds, c, level):
    return jnp.concatenate([winds[c, 2 * level], winds[c, 2 * level + 1]], -1)


def step_kernel(
    mean_h, lon_h, lat_h, zon_h, mer_h, mix_h, flux_h, region_h, scaling_h, reader_h,
    cells,
    mix_v, flux_v, region_v, scaling_s, reader_s, got_u, got_v, got_spare_u, got_spare_v, mine, theirs, slips, slips_in,
    winds, beyond, pack, halo, edge, south, last, north,
    in_sem, own_sem, scatter_send, scatter_recv, swap_send, swap_recv, slip_send, slip_recv, gather_send, gather_recv,
    halo_send, halo_recv, late, beside,
):
    band, me = lax.axis_index("band"), lax.axis_index("member")
    bands = lax.axis_size("band")
    line = (me // 2) % 2
    place = me // 4 * 2 + me % 2
    got = ((got_u, got_v), (got_spare_u, got_spare_v))
    has_south, has_north = band > 0, band < bands - 1
    around = has_south.astype(jnp.int32) + has_north.astype(jnp.int32)
    tail_end = me == 0
    answers = jnp.logical_and(tail_end, band % 2 == 0)
    owns = place != 0
    owns_spare = place == 1
    partner = me + 2 - 4 * line

    def member(where, which):
        return (where // 2 * 2 + which) * 2 + where % 2

    loads = [
        pltpu.make_async_copy(mix_h, mix_v, in_sem.at[3]),
        pltpu.make_async_copy(flux_h, flux_v, in_sem.at[4]),
        pltpu.make_async_copy(region_h, region_v, in_sem.at[5]),
        pltpu.make_async_copy(scaling_h, scaling_s, in_sem.at[6]),
        pltpu.make_async_copy(mean_h.at[0], cells.at[0], in_sem.at[0]),
        pltpu.make_async_copy(lon_h.at[0], cells.at[1], in_sem.at[1]),
        pltpu.make_async_copy(lat_h.at[0], cells.at[2], in_sem.at[2]),
    ]
    load_reader = pltpu.make_async_copy(reader_h, reader_s, in_sem.at[7])

    def signal_beside(semaphore, who):
        for there, step in ((has_south, -1), (has_north, 1)):
            @pl.when(there)
            def _():
                pl.semaphore_signal(semaphore, inc=1, device_id=(band + step, who), device_id_type=MESH)

    def signal_line(semaphore):
        for step in range(1, LINE):
            target = member((place + step) % LINE, line)
            pl.semaphore_signal(semaphore, inc=1, device_id=(band, target), device_id_type=MESH)

    barrier = pltpu.get_barrier_semaphore()

    @pl.when(jnp.logical_not(tail_end))
    def _():
        signal_line(barrier)

    @pl.when(owns)
    def _():
        pl.semaphore_signal(barrier, inc=1, device_id=(band, partner), device_id_type=MESH)
        signal_beside(barrier, partner)

    pl.when(jnp.logical_not(answers))(lambda: signal_beside(barrier, me))
    in_line = jnp.where(jnp.logical_and(line == 0, owns), LINE - 2, LINE - 1)
    outside = jnp.where(owns, 1 + 2 * around, jnp.where(jnp.logical_or(answers, me == 2), around, 0))
    pl.semaphore_wait(barrier, in_line + outside)

    def piece(c, there):
        return (mer_h if c else zon_h).at[0, there // 2, :, pl.ds(pl.multiple_of(there % 2 * HALF, HALF), HALF)]

    for c in range(2):
        for step in (4, 5, 3, 2, 6, 7, 1, 0):
            there = (place + step) % LINE
            for spare in range(2):
                def send():
                    pltpu.make_async_remote_copy(
                        src_ref=piece(c, there), dst_ref=got[spare][c].at[place], send_sem=scatter_send,
                        recv_sem=scatter_recv.at[spare, c], device_id=(band, member(jnp.maximum(there, 1), line)),
                        device_id_type=MESH,
                    ).start()

                def keep():
                    pltpu.make_async_copy(piece(c, there), got[spare][c].at[place], own_sem.at[spare, c]).start()

                fits = there == 0 if spare else there != 0
                if step in (0, 7):
                    pl.when(jnp.logical_and(fits, jnp.maximum(there, 1) == place))(keep)
                    pl.when(jnp.logical_and(fits, jnp.maximum(there, 1) != place))(send)
                else:
                    pl.when(fits)(send)

    pl.when(tail_end)(lambda: signal_line(late))

    load_reader.start()
    for load in loads:
        load.start()

    pl.when(answers)(lambda: signal_beside(beside, me))

    for load in loads[:4]:
        load.wait()
    region = region_v[...]
    weight = jnp.zeros(region.shape, jnp.float32)
    for code in range(REGIONS):
        weight = jnp.where(region == code, scaling_s[0, code], weight)
    land = jnp.where(region < REGIONS // 2, 1.0, 0.4)
    emission = 0.5 * flux_v[...] * land * weight
    zero = jnp.zeros_like(emission)
    below = [zero] + [mix_v[level] for level in range(LEVELS - 1)]
    above = below[1:] + [zero]
    ratios, inverse = [], []
    for level in range(LEVELS):
        denom = 1.0 + below[level] + above[level]
        if level:
            denom = denom + below[level] * ratios[-1]
        inverse.append(1.0 / denom)
        ratios.append(-above[level] * inverse[-1])
    for load in loads[4:]:
        load.wait()
    for k in range(3):
        values = []
        for level in range(LEVELS):
            source = cells[k, level]
            if k == 0 and level == 0:
                source = source + emission
            if level:
                source = source + below[level] * values[-1]
            values.append(source * inverse[level])
        result = values[-1]
        for level in range(LEVELS - 1, -1, -1):
            if level < LEVELS - 1:
                result = values[level] - ratios[level] * result
            cells[k, level] = result
            pack[0, k, pl.ds(2 * level, 2), :] = result[:2]
            pack[1, k, pl.ds(2 * level, 2), :] = result[ROWS - 2:]

    def across(side):
        return pltpu.make_async_remote_copy(
            src_ref=pack.at[side], dst_ref=halo.at[1 - side, pl.ds(0, 3)],
            send_sem=halo_send.at[side], recv_sem=halo_recv.at[1 - side],
            device_id=(band + (1 if side else -1), me), device_id_type=MESH,
        )

    sides = ((0, has_south), (1, has_north))

    load_reader.wait()

    @pl.when(jnp.logical_and(tail_end, jnp.logical_not(answers)))
    def _():
        pl.semaphore_wait(beside, around)

    for side, there in sides:
        pl.when(there)(across(side).start)

    def arrive(spare, c):
        kept = got[spare][c].at[place]
        pltpu.make_async_copy(kept, kept, own_sem.at[spare, c]).wait()
        part = got[spare][c].at[pl.ds(0, LINE - 1)]
        pltpu.make_async_copy(part, part, scatter_recv.at[spare, c]).wait()

    reader = reader_s[0]
    here = (reader // 2) % 2 == line
    reader_place = reader // 4 * 2 + reader % 2

    def swap(spare, c):
        return pltpu.make_async_remote_copy(
            src_ref=mine.at[spare, c], dst_ref=theirs.at[spare, c], send_sem=swap_send.at[spare, c],
            recv_sem=swap_recv.at[spare, c], device_id=(band, partner), device_id_type=MESH,
        )

    def slip(spare, c, side, other):
        return pltpu.make_async_remote_copy(
            src_ref=slips.at[spare, c, side], dst_ref=slips_in.at[spare, c, 1 - side, other],
            send_sem=slip_send.at[spare, c, side, other], recv_sem=slip_recv.at[spare, c, 1 - side, other],
            device_id=(band + (1 if side else -1), partner if other else me), device_id_type=MESH,
        )

    def offer(spare, c):
        chosen = got[spare][c][reader_place]
        mine[spare, c] = chosen
        swap(spare, c).start()
        slips[spare, c, 0] = jnp.where(here, chosen[:2], 0.0)
        slips[spare, c, 1] = jnp.where(here, chosen[ROWS - 2:], 0.0)
        for side, there in sides:
            for other in (1, 0):
                pl.when(there)(slip(spare, c, side, other).start)

    def share(ref, part, c, whose):
        for step in (4, 5, 3, 2, 6, 7, 1):
            target = member((place + step) % LINE, line)
            pltpu.make_async_remote_copy(
                src_ref=ref.at[c, whose], dst_ref=ref.at[c, whose], send_sem=gather_send.at[part, c],
                recv_sem=gather_recv.at[part, c], device_id=(band, target), device_id_type=MESH,
            ).start()

    def settle(spare, c):
        swap(spare, c).wait_recv()
        whose = 0 if spare else place
        winds[c, whose] = jnp.where(here, mine[spare, c], theirs[spare, c])
        share(winds, 0, c, whose)

    def settle_beside(spare, c):
        whose = 0 if spare else place
        for side, there in sides:
            @pl.when(there)
            def _():
                for other in range(2):
                    slip(spare, c, 1 - side, other).wait_recv()
                both = slips_in[spare, c, side, 0] + slips_in[spare, c, side, 1]
                beyond[c, whose, pl.ds(2 * side, 2), :] = both

            @pl.when(jnp.logical_not(there))
            def _():
                beyond[c, whose, pl.ds(2 * side, 2), :] = jnp.zeros((2, HALF), jnp.float32)

        share(beyond, 1, c, whose)

    @pl.when(owns)
    def _():
        for c in range(2):
            arrive(0, c)
            offer(0, c)

            @pl.when(owns_spare)
            def _():
                arrive(1, c)
                offer(1, c)

        @pl.when(line == 0)
        def _():
            pl.semaphore_wait(late, 1)

        for c in range(2):
            settle(0, c)
            pl.when(owns_spare)(lambda: settle(1, c))
            settle_beside(0, c)
            pl.when(owns_spare)(lambda: settle_beside(1, c))

    def await_winds(ref, part, c):
        cases = ((0, jnp.logical_not(owns)), (1, jnp.logical_and(owns, jnp.logical_not(owns_spare))), (2, owns_spare))
        for owned, case in cases:
            @pl.when(case)
            def _():
                some = ref.at[c, pl.ds(0, LINE - owned)]
                pltpu.make_async_copy(some, some, gather_recv.at[part, c]).wait()

    def halo_wind(c):
        await_winds(beyond, 1, c)
        for there in range(LINE):
            for side in range(2):
                place_rows = (pl.ds(there // 2 * 2, 2), pl.ds(there % 2 * HALF, HALF))
                halo[side, 3 + c, *place_rows] = beyond[c, there, pl.ds(2 * side, 2), :]

    row = lax.broadcasted_iota(jnp.int32, (ROWS, LONS), 0)
    order = (0, 2, 1)

    def up(x):
        return pltpu.roll(x, 1, 0)

    def down(x):
        return pltpu.roll(x, ROWS - 1, 0)

    def meridional(c):
        return (c[0], c[2], c[1])

    no_south, no_north = jnp.logical_not(has_south), jnp.logical_not(has_north)
    for sub in range(SUB):
        if sub == 0:
            await_winds(winds, 0, 0)
        for level in range(LEVELS):
            swept = zonal(tuple(cells[k, level] for k in range(3)), wind_of(winds, 0, level))
            for k in range(3):
                cells[k, level] = swept[k]
                edge[k, pl.ds(2 * level, 1), :] = swept[k][ROWS - 1:]
                edge[k, pl.ds(2 * level + 1, 1), :] = swept[k][:1]
        if sub == 0:
            for side, there in sides:
                @pl.when(there)
                def _():
                    across(1 - side).wait_recv()

                @pl.when(jnp.logical_not(there))
                def _():
                    halo[side, pl.ds(0, 3)] = jnp.zeros((3, ROWS, LONS), jnp.float32)

            halo_wind(0)
            s_cells = tuple(halo[0, k] for k in range(3))
            n_cells = tuple(halo[1, k] for k in range(3))
        edges = tuple(edge[k] for k in range(3))
        s_cells = tuple(jnp.where(no_south, e, x) for e, x in zip(edges, zonal(s_cells, halo[0, 3])))
        n_cells = tuple(jnp.where(no_north, e, x) for e, x in zip(edges, zonal(n_cells, halo[1, 3])))
        s_mer, n_mer, e_mer = meridional(s_cells), meridional(n_cells), meridional(edges)
        if sub == 0:
            await_winds(winds, 0, 1)
            halo_wind(1)
            v_north = jnp.where(no_north, 0.0, halo[1, 4])
            for level in range(LEVELS):
                edge[3, pl.ds(2 * level + 1, 1), :] = wind_of(winds, 1, level)[:1]
                edge[3, pl.ds(2 * level, 1), :] = jnp.zeros((1, LONS), jnp.float32)
        flux_8 = upwind(v_north, e_mer, n_mer)
        for k in range(3):
            south[k] = s_mer[k]
            last[k] = flux_8[k]
        north[...] = n_cells[0]
        if sub < SUB - 1:
            flux_m1 = upwind(halo[0, 4], tuple(up(x) for x in s_mer), s_mer)
            flux_0 = upwind(edge[3], s_mer, e_mer)
            s_cells = meridional(advance(s_mer, flux_m1, flux_0, up(s_mer[0]), e_mer[0]))
            flux_9 = upwind(down(v_north), n_mer, tuple(down(x) for x in n_mer))
            n_cells = meridional(advance(n_mer, flux_8, flux_9, e_mer[0], down(n_mer[0])))
        for level in range(LEVELS):
            faces = jnp.where(jnp.logical_and(row == 0, no_south), 0.0, wind_of(winds, 1, level))
            now = tuple(cells[k, level] for k in order)
            left = tuple(
                jnp.where(row == 0, south[k, pl.ds(2 * level + 1, 1), :], up(x)) for k, x in enumerate(now)
            )
            flux = upwind(faces, left, now)
            flux_next = tuple(
                jnp.where(row == ROWS - 1, last[k, pl.ds(2 * level, 1), :], down(x)) for k, x in enumerate(flux)
            )
            mean_next = jnp.where(row == ROWS - 1, north[pl.ds(2 * level, 1), :], down(now[0]))
            new = advance(now, flux, flux_next, left[0], mean_next)
            for k, value in zip(order, new):
                cells[k, level] = value

    def drain(ref, count, semaphore):
        some = ref.at[pl.ds(0, count)]
        pltpu.make_async_copy(some, some, semaphore).wait()

    def drain_owner(spare, c):
        swap(spare, c).wait_send()
        for side, there in sides:
            for other in range(2):
                pl.when(there)(slip(spare, c, side, other).wait_send)
        for part, ref in enumerate((winds, beyond)):
            drain(ref.at[c], LINE - 1, gather_send.at[part, c])

    for c in range(2):
        drain(got_u, LINE - 2, scatter_send)
        pl.when(jnp.logical_not(owns))(lambda: drain(got_u, 2, scatter_send))

        @pl.when(owns)
        def _():
            drain_owner(0, c)
            pl.when(owns_spare)(lambda: drain_owner(1, c))
            pl.when(jnp.logical_not(owns_spare))(lambda: drain(got_u, 1, scatter_send))

    for side, there in sides:
        pl.when(there)(across(side).wait_send)


def store_kernel(cells, out_mean, out_lon, out_lat, out_sem):
    stores = [
        pltpu.make_async_copy(cells.at[k], out.at[0], out_sem.at[k]) for k, out in enumerate((out_mean, out_lon, out_lat))
    ]
    for store in stores:
        store.start()
    for store in stores:
        store.wait()


def on_device(*args):
    hbm = pl.BlockSpec(memory_space=pl.ANY)
    local = pl.BlockSpec(memory_space=pltpu.VMEM)
    dma, regular = pltpu.SemaphoreType.DMA, pltpu.SemaphoreType.REGULAR

    def vmem(*dims):
        return pltpu.VMEM(dims, jnp.float32)

    cells = pl.pallas_call(
        step_kernel,
        out_shape=vmem(3, LEVELS, ROWS, LONS),
        in_specs=[hbm] * 10,
        out_specs=local,
        scratch_shapes=[
            vmem(LEVELS - 1, ROWS, LONS),
            vmem(ROWS, LONS),
            pltpu.VMEM((ROWS, LONS), jnp.int32),
            pltpu.SMEM((1, REGIONS), jnp.float32),
            pltpu.SMEM((1,), jnp.int32),
            *[vmem(LINE, ROWS, HALF)] * 4,
            vmem(2, 2, ROWS, HALF),
            vmem(2, 2, ROWS, HALF),
            vmem(2, 2, 2, 2, HALF),
            vmem(2, 2, 2, 2, 2, HALF),
            vmem(2, LINE, ROWS, HALF),
            vmem(2, LINE, 4, HALF),
            vmem(2, 3, ROWS, LONS),
            vmem(2, 5, ROWS, LONS),
            vmem(4, ROWS, LONS),
            vmem(3, ROWS, LONS),
            vmem(3, ROWS, LONS),
            vmem(ROWS, LONS),
            dma((8,)), dma((2, 2)), dma, dma((2, 2)), dma((2, 2)), dma((2, 2)), dma((2, 2, 2, 2)), dma((2, 2, 2, 2)),
            dma((2, 2)), dma((2, 2)), dma((2,)), dma((2,)), regular, regular,
        ],
        compiler_params=pltpu.CompilerParams(collective_id=0, has_side_effects=True),
    )(*args)
    return pl.pallas_call(
        store_kernel,
        out_shape=(jax.ShapeDtypeStruct(args[0].shape, jnp.float32),) * 3,
        in_specs=[local],
        out_specs=(hbm,) * 3,
        scratch_shapes=[dma((3,))],
    )(pltpu.with_memory_space_constraint(cells, pltpu.VMEM))


def solution(mesh):
    moments = P("member", None, "band", None)
    return jax.shard_map(
        on_device,
        mesh=mesh,
        in_specs=(
            moments, moments, moments, moments, moments,
            P(None, "band", None),
            P("band", None),
            P("band", None),
            P("member", None),
            P("band"),
        ),
        out_specs=(moments,) * 3,
        check_vma=False,
    )
```

time: 23.2 us -> 22.7 us (0.978)
  the two profiles are of different devices: /device:TPU:384 before, /device:TPU:225 now
where the time goes in v5:
time: 22.7 us; the launch traced here: 22.6 us
  Pallas kernels  21.3 us (94%)
  between operations  1.29 us (6%)
    pallas_call x1, Pallas kernels, on_device(): pl.pallas_call(step_kernel, out_shape=vmem(3, LEVELS, ROWS, LONS), in_spe...  20.5 us
    pallas_call x1, Pallas kernels, on_device(): pl.pallas_call(store_kernel, out_shape=(jax.ShapeDtypeStruct(args[0].shap...  0.73 us

profile of v5, /device:TPU:225, one launch (start us, length us, event | category | flops | bytes accessed | tf_op | source)
XLA Modules:
  0.0 22.6 jit_solution(3755973232719009919)
XLA Ops:
  1.3 20.5 %shard_map.121.cells = f32[3,4,8,768]{3,2,1,0:T(8,128)S(1)} custom-call(f32[1,4,8,768]{3,2,1,0:T(8,128)} %mean_h.1, f32[1,4,8,768]{3,2,1,0:T(8,128)} %lon_h.1, f32[1,4,8,768]{3,2,1,0:T(8,128)} %lat_h.1, f32[1,4,8,768]{3,2,1,0:T(8,128)} %zon_h.1, f32[1,4,8,768]{3,2,1,0:T(8,128)} %mer_h.1, f32[3,8,768]{2,1,0:T(8,128)} %mix_h.1, f32[8,768]{1,0:T(8,128)} %flux_h.1, ...), custom_call_target="tpu_custom_call" | custom-call | tf_op jit(solution)/shard_map/pallas_call | solution.py:406
  21.8 0.7 %shard_map.122 = (f32[1,4,8,768]{3,2,1,0:T(8,128)}, f32[1,4,8,768]{3,2,1,0:T(8,128)}, f32[1,4,8,768]{3,2,1,0:T(8,128)}) custom-call(f32[3,4,8,768]{3,2,1,0:T(8,128)S(1)} %shard_map.121.cells), custom_call_target="tpu_custom_call" | custom-call | tf_op jit(solution)/shard_map/pallas_call | solution.py:435

commit v6 on v5

--- a/solution.py
+++ b/solution.py
@@ -42,7 +42,7 @@
 def step_kernel(
     mean_h, lon_h, lat_h, zon_h, mer_h, mix_h, flux_h, region_h, scaling_h, reader_h,
     cells,
-    mix_v, flux_v, region_v, scaling_s, reader_s, got_u, got_v, got_spare_u, got_spare_v, mine, theirs, slips, slips_in,
+    mix_v, flux_v, region_v, scaling_s, reader_s, slab, got_u, got_v, got_spare_u, got_spare_v, mine, theirs, slips, slips_in,
     winds, beyond, pack, halo, edge, south, last, north,
     in_sem, own_sem, scatter_send, scatter_recv, swap_send, swap_recv, slip_send, slip_recv, gather_send, gather_recv,
     halo_send, halo_recv, late, beside,
@@ -72,6 +72,10 @@
         pltpu.make_async_copy(lon_h.at[0], cells.at[1], in_sem.at[1]),
         pltpu.make_async_copy(lat_h.at[0], cells.at[2], in_sem.at[2]),
     ]
+    slab_loads = [
+        pltpu.make_async_copy(zon_h.at[0], slab.at[0], in_sem.at[8]),
+        pltpu.make_async_copy(mer_h.at[0], slab.at[1], in_sem.at[9]),
+    ]
     load_reader = pltpu.make_async_copy(reader_h, reader_s, in_sem.at[7])
 
     def signal_beside(semaphore, who):
@@ -97,42 +101,52 @@
         signal_beside(barrier, partner)
 
     pl.when(jnp.logical_not(answers))(lambda: signal_beside(barrier, me))
-    in_line = jnp.where(jnp.logical_and(line == 0, owns), LINE - 2, LINE - 1)
-    outside = jnp.where(owns, 1 + 2 * around, jnp.where(jnp.logical_or(answers, me == 2), around, 0))
-    pl.semaphore_wait(barrier, in_line + outside)
-
-    def piece(c, there):
-        return (mer_h if c else zon_h).at[0, there // 2, :, pl.ds(pl.multiple_of(there % 2 * HALF, HALF), HALF)]
-
-    for c in range(2):
-        for step in (4, 5, 3, 2, 6, 7, 1, 0):
-            there = (place + step) % LINE
-            for spare in range(2):
-                def send():
-                    pltpu.make_async_remote_copy(
-                        src_ref=piece(c, there), dst_ref=got[spare][c].at[place], send_sem=scatter_send,
-                        recv_sem=scatter_recv.at[spare, c], device_id=(band, member(jnp.maximum(there, 1), line)),
-                        device_id_type=MESH,
-                    ).start()
-
-                def keep():
-                    pltpu.make_async_copy(piece(c, there), got[spare][c].at[place], own_sem.at[spare, c]).start()
-
-                fits = there == 0 if spare else there != 0
-                if step in (0, 7):
-                    pl.when(jnp.logical_and(fits, jnp.maximum(there, 1) == place))(keep)
-                    pl.when(jnp.logical_and(fits, jnp.maximum(there, 1) != place))(send)
-                else:
-                    pl.when(fits)(send)
-
-    pl.when(tail_end)(lambda: signal_line(late))
+    def enter(tail_end_here):
+        in_line = jnp.where(jnp.logical_and(line == 0, owns), LINE - 2, LINE - 1)
+        outside = jnp.where(owns, 1 + 2 * around, jnp.where(jnp.logical_or(answers, me == 2), around, 0))
+        pl.semaphore_wait(barrier, in_line + outside)
+
+        def piece(c, there):
+            field = (mer_h if c else zon_h).at[0] if tail_end_here else slab.at[c]
+            return field.at[there // 2, :, pl.ds(pl.multiple_of(there % 2 * HALF, HALF), HALF)]
+
+        for c in range(2):
+            for step in (4, 5, 3, 2, 6, 7, 1, 0):
+                there = (place + step) % LINE
+                for spare in range(2):
+                    def send():
+                        pltpu.make_async_remote_copy(
+                            src_ref=piece(c, there), dst_ref=got[spare][c].at[place], send_sem=scatter_send,
+                            recv_sem=scatter_recv.at[spare, c], device_id=(band, member(jnp.maximum(there, 1), line)),
+                            device_id_type=MESH,
+                        ).start()
+
+                    def keep():
+                        pltpu.make_async_copy(piece(c, there), got[spare][c].at[place], own_sem.at[spare, c]).start()
+
+                    fits = there == 0 if spare else there != 0
+                    if step in (0, 7):
+                        pl.when(jnp.logical_and(fits, jnp.maximum(there, 1) == place))(keep)
+                        pl.when(jnp.logical_and(fits, jnp.maximum(there, 1) != place))(send)
+                    else:
+                        pl.when(fits)(send)
+
+    for load in loads[:7]:
+        load.start()
+
+    @pl.when(tail_end)
+    def _():
+        enter(True)
+        signal_line(late)
+
+    pl.when(answers)(lambda: signal_beside(beside, me))
+
+    @pl.when(jnp.logical_not(tail_end))
+    def _():
+        for load in slab_loads:
+            load.start()
 
     load_reader.start()
-    for load in loads:
-        load.start()
-
-    pl.when(answers)(lambda: signal_beside(beside, me))
-
     for load in loads[:4]:
         load.wait()
     region = region_v[...]
@@ -169,6 +183,13 @@
             cells[k, level] = result
             pack[0, k, pl.ds(2 * level, 2), :] = result[:2]
             pack[1, k, pl.ds(2 * level, 2), :] = result[ROWS - 2:]
+
+
+    @pl.when(jnp.logical_not(tail_end))
+    def _():
+        for load in slab_loads:
+            load.wait()
+        enter(False)
 
     def across(side):
         return pltpu.make_async_remote_copy(
@@ -414,6 +435,7 @@
             pltpu.VMEM((ROWS, LONS), jnp.int32),
             pltpu.SMEM((1, REGIONS), jnp.float32),
             pltpu.SMEM((1,), jnp.int32),
+            vmem(2, LEVELS, ROWS, LONS),
             *[vmem(LINE, ROWS, HALF)] * 4,
             vmem(2, 2, ROWS, HALF),
             vmem(2, 2, ROWS, HALF),
@@ -427,7 +449,7 @@
             vmem(3, ROWS, LONS),
             vmem(3, ROWS, LONS),
             vmem(ROWS, LONS),
-            dma((8,)), dma((2, 2)), dma, dma((2, 2)), dma((2, 2)), dma((2, 2)), dma((2, 2, 2, 2)), dma((2, 2, 2, 2)),
+            dma((10,)), dma((2, 2)), dma, dma((2, 2)), dma((2, 2)), dma((2, 2)), dma((2, 2, 2, 2)), dma((2, 2, 2, 2)),
             dma((2, 2)), dma((2, 2)), dma((2,)), dma((2,)), regular, regular,
         ],
         compiler_params=pltpu.CompilerParams(collective_id=0, has_side_effects=True),

time: 22.7 us -> 22.2 us (0.978)
  the two profiles are of different devices: /device:TPU:225 before, /device:TPU:384 now
where the time goes in v6:
time: 22.2 us; the launch traced here: 21.9 us
  Pallas kernels  20.6 us (93%)
  between operations  1.29 us (6%)
    pallas_call x1, Pallas kernels, on_device(): pl.pallas_call(step_kernel, out_shape=vmem(3, LEVELS, ROWS, LONS), in_spe...  19.8 us
    pallas_call x1, Pallas kernels, on_device(): pl.pallas_call(store_kernel, out_shape=(jax.ShapeDtypeStruct(args[0].shap...  0.73 us

profile of v6, /device:TPU:384, one launch (start us, length us, event | category | flops | bytes accessed | tf_op | source)
XLA Modules:
  0.0 21.9 jit_solution(17755516188380772577)
XLA Ops:
  1.3 19.8 %shard_map.121.cells = f32[3,4,8,768]{3,2,1,0:T(8,128)S(1)} custom-call(f32[1,4,8,768]{3,2,1,0:T(8,128)} %mean_h.1, f32[1,4,8,768]{3,2,1,0:T(8,128)} %lon_h.1, f32[1,4,8,768]{3,2,1,0:T(8,128)} %lat_h.1, f32[1,4,8,768]{3,2,1,0:T(8,128)} %zon_h.1, f32[1,4,8,768]{3,2,1,0:T(8,128)} %mer_h.1, f32[3,8,768]{2,1,0:T(8,128)} %mix_h.1, f32[8,768]{1,0:T(8,128)} %flux_h.1, ...), custom_call_target="tpu_custom_call" | custom-call | tf_op jit(solution)/shard_map/pallas_call | solution.py:427
  21.1 0.7 %shard_map.122 = (f32[1,4,8,768]{3,2,1,0:T(8,128)}, f32[1,4,8,768]{3,2,1,0:T(8,128)}, f32[1,4,8,768]{3,2,1,0:T(8,128)}) custom-call(f32[3,4,8,768]{3,2,1,0:T(8,128)S(1)} %shard_map.121.cells), custom_call_target="tpu_custom_call" | custom-call | tf_op jit(solution)/shard_map/pallas_call | solution.py:457
